TPU v7x, 128 devices: a whole 4x4x4 slice. The times are simulated.
128 devices in a mesh: samp: 8 (over y, core), snp: 16 (over z, x).
Axes of the slice: x: 4, y: 4, z: 4, core: 2. Of those that a mesh axis runs over, the one named last changes fastest.
Arguments:
- genotypes: int32 [24576, 22528], P('samp', 'snp'), may hold values from 0 to 2, as said below
- allele_counts: int32 [22528], P('snp'), may hold values from 2 to 49150, as said below
- ridge_delta: float32 [4], replicated, may hold values from 0.3 to 3
- solution: float32 [4, 24576], P(None, ('samp', 'snp')), may hold values from -6 to 6
- residual: float32 [4, 24576], P(None, ('samp', 'snp')), may hold values from -6 to 6
- direction: float32 [4, 24576], P(None, ('samp', 'snp')), may hold values from -6 to 6
Outputs:
- solution_out: float32 [4, 24576], P(None, ('samp', 'snp'))
- residual_out: float32 [4, 24576], P(None, ('samp', 'snp'))
- direction_out: float32 [4, 24576], P(None, ('samp', 'snp'))
Inputs may be any that keep to these rules, and one draw needn't show every extreme that they name: `genotypes`: every SNP has at least one sample of dosage 0 and at least one of dosage 2. allele_counts[j] is the sum of genotypes[:, j] over all 24576 samples.
All inputs are finite; a program needn't handle non-finite values.
Results may differ from a plain program's by a relative error of at most 0.0003.
Values sent between devices are 32-bit elements; how exact they have to be, the bound alone decides.
No kernel may reach another device: no remote copies, remote signals or barrier semaphores. Data moves between devices by JAX's collectives and lax.ppermute only.
A program may use at most 128 MiB of HBM per device.

v0:
```python
import functools

import jax
import jax.numpy as jnp
from jax import lax
from jax.experimental import pallas as pl
from jax.experimental.pallas import tpu as pltpu
from jax.sharding import PartitionSpec as P

ITERS = 3
LANES = 128
TILE = 256
STEP_ROWS = 256
BF16 = jnp.bfloat16
F32 = jnp.float32
VMEM_BYTES = 12 * 2**20


def split(v):
    high = v.astype(BF16).astype(F32)
    rest = v - high
    middle = rest.astype(BF16).astype(F32)
    parts = [high, middle, rest - middle, jnp.zeros_like(v)]
    return jnp.concatenate(parts, axis=0).astype(BF16)


def join(raw):
    return raw[0:4] + (raw[4:8] + raw[8:12])


def lanes_of(*columns):
    lane = lax.broadcasted_iota(jnp.int32, (columns[0].shape[0], LANES), 1)
    block = jnp.zeros(lane.shape, F32)
    for i, column in enumerate(columns):
        block = jnp.where(lane == i, column, block)
    return block


def total(v):
    return jnp.sum(v, axis=1, keepdims=True)


def forward(v, upper, lower, stats, out):
    parts = split(v)
    shift = total(v)
    half, snps = upper.shape
    for n in range(0, snps, TILE):
        at = slice(n, min(n + TILE, snps))
        raw = jnp.dot(parts[:, :half], upper[:, at], preferred_element_type=F32)
        raw += jnp.dot(parts[:, half:], lower[:, at], preferred_element_type=F32)
        out[:, at] = (join(raw) - shift * stats[0:1, at]) * stats[1:2, at]


def backward(u, upper, lower, stats, out):
    w = u * stats[1:2, :]
    parts = split(w)
    shift = total(w * stats[0:1, :])
    half = upper.shape[1]
    for start, turned in ((0, upper), (half, lower)):
        for n in range(0, half, TILE):
            raw = jnp.dot(parts, turned[:, n : n + TILE], preferred_element_type=F32)
            out[:, start + n : start + n + TILE] = join(raw) - shift


def convert_kernel(part, genotypes, dosage, landed, arrived):
    blocks = landed.shape[0]

    def copy(block):
        rows = pl.ds((part * blocks + block) * STEP_ROWS, STEP_ROWS)
        return pltpu.make_async_copy(genotypes.at[rows, :], landed.at[block], arrived.at[block])

    for block in range(blocks):
        copy(block).start()
    for block in range(blocks):
        copy(block).wait()
        rows = slice(block * STEP_ROWS, (block + 1) * STEP_ROWS)
        dosage[rows, :] = landed[block].astype(F32).astype(BF16)


def stats_kernel(alleles, counts, stats):
    freq = counts[...].reshape(1, counts.shape[0]).astype(F32) / alleles
    stats[0:1, :] = 2.0 * freq
    stats[1:2, :] = 1.0 / jnp.sqrt(2.0 * freq * (1.0 - freq))
    stats[2:8, :] = jnp.zeros((6, freq.shape[1]), F32)


def turn_kernel(dosage, turned):
    rows, snps = dosage.shape
    for m in range(0, rows, 2 * TILE):
        for n in range(0, snps, LANES):
            turned[n : n + LANES, m : m + 2 * TILE] = dosage[m : m + 2 * TILE, n : n + LANES].T


def first_forward_kernel(own, one, two, three, upper, lower, stats, r, d, out):
    z, x = lax.axis_index("z"), lax.axis_index("x")
    piece = own.shape[1]
    for k, ref in enumerate((own, one, two, three)):
        at = pl.ds(pl.multiple_of(lax.rem(z + k, 4) * piece, LANES), piece)
        block = pltpu.roll(ref[...], x * (piece // 4), 1)
        r[:, at] = block[0:4]
        d[:, at] = block[4:8]
    snps = upper.shape[1]
    forward(d[...], upper, lower, stats, out)
    out[:, snps:] = lanes_of(total(r[...] * r[...]), total(d[...] * d[...]))


def first_backward_kernel(sums, upper, lower, stats, u, scalars, out):
    snps, half = upper.shape
    u[...] = sums[:, :snps]
    scalars[...] = sums[:, snps:]
    backward(u[...], upper, lower, stats, out)
    out[:, 2 * half :] = lanes_of(total(u[...] * u[...]))


def advance(snps_all, sums, ridge, scalars, r, d, moved):
    rows = r.shape[1]
    norm, size = scalars[:, 0:1], scalars[:, 1:2]
    delta = ridge[:, 0:1]
    curve = sums[:, rows : rows + 1] / snps_all + delta * size
    step = norm / curve
    r_new = r[...] - step * (sums[:, :rows] / snps_all + delta * d[...])
    moved_new = step * d[...]
    if moved is not None:
        moved_new = moved[...] + moved_new
    return r_new, moved_new


def forward_kernel(snps_all, first, *refs):
    sums, ridge, scalars, r, d = refs[:5]
    moved = None if first else refs[5]
    upper, lower, stats, r_out, moved_out, out = refs[5 if first else 6 :]
    r_new, moved_out[...] = advance(snps_all, sums, ridge, scalars, r, d, moved)
    r_out[...] = r_new
    snps = upper.shape[1]
    forward(r_new, upper, lower, stats, out)
    out[:, snps:] = lanes_of(total(r_new * r_new), total(r_new * d[...]))


def backward_kernel(sums, u, r, d, scalars, upper, lower, stats, u_out, d_out, scalars_out, out):
    snps, half = upper.shape
    norm, size = scalars[:, 0:1], scalars[:, 1:2]
    norm_next, cross = sums[:, snps : snps + 1], sums[:, snps + 1 : snps + 2]
    ratio = norm_next / norm
    u_new = sums[:, :snps] + ratio * u[...]
    u_out[...] = u_new
    d_out[...] = r[...] + ratio * d[...]
    scalars_out[...] = lanes_of(norm_next, norm_next + 2.0 * ratio * cross + ratio * ratio * size)
    backward(u_new, upper, lower, stats, out)
    out[:, 2 * half :] = lanes_of(total(u_new * u_new))


def last_kernel(snps_all, sums, ridge, scalars, r, d, moved, r_out, moved_out, norm):
    r_new, moved_out[...] = advance(snps_all, sums, ridge, scalars, r, d, moved)
    r_out[...] = r_new
    norm[...] = lanes_of(total(r_new * r_new))


def own_kernel(r, d, moved, solution, s_out, r_out, d_out, r_keep):
    rows, own = r.shape[1], solution.shape[1]
    back = rows - (lax.axis_index("z") * lax.axis_size("x") + lax.axis_index("x")) * own
    s_out[...] = solution[...] + pltpu.roll(moved[...], back, 1)[:, :own]
    mine = pltpu.roll(r[...], back, 1)[:, :own]
    r_out[...] = mine
    r_keep[...] = mine
    d_out[...] = pltpu.roll(d[...], back, 1)[:, :own]


def call(kernel, outs, *args, name, dtypes=None, flops=0):
    spec = pl.BlockSpec(memory_space=pltpu.VMEM)
    return pl.pallas_call(
        kernel,
        out_shape=[jax.ShapeDtypeStruct(s, t) for s, t in zip(outs, dtypes or [F32] * len(outs))],
        in_specs=[spec] * len(args),
        out_specs=[spec] * len(outs),
        compiler_params=pltpu.CompilerParams(vmem_limit_bytes=VMEM_BYTES),
        cost_estimate=pl.CostEstimate(flops=flops, bytes_accessed=2**20, transcendentals=0),
        name=name,
    )(*args)


def from_next(value, axis, k):
    size = lax.axis_size(axis)
    return lax.ppermute(value, axis, [((i + k) % size, i) for i in range(size)])


def others(value, axis):
    return [from_next(value, axis, k) for k in range(1, lax.axis_size(axis))]


def sum_over(value, axis):
    size = lax.axis_size(axis)
    swapped = [lax.ppermute(value, axis, [(i, i ^ k) for i in range(size)]) for k in (1, 3, 2)]
    return (value + swapped[0]) + (swapped[1] + swapped[2])


def local(genotypes, allele_counts, ridge, solution, residual, direction):
    rows, snps = genotypes.shape
    k, own = solution.shape
    samples_all = rows * lax.axis_size("y") * lax.axis_size("c")
    snps_all = snps * lax.axis_size("z") * lax.axis_size("x")
    ridge = jnp.broadcast_to(ridge[:, None], (ridge.shape[0], LANES))
    flops = 2 * 16 * rows * snps
    full, short = (k, rows + LANES), (k, snps + LANES)
    vec, row, col, mine = (k, rows), (k, snps), (k, LANES), (k, own)

    half = rows // 2
    steps = half // STEP_ROWS
    genotypes = pltpu.with_memory_space_constraint(genotypes, pltpu.HBM)

    def converted(part):
        return pl.pallas_call(
            functools.partial(convert_kernel, part),
            out_shape=jax.ShapeDtypeStruct((half, snps), BF16),
            in_specs=[pl.BlockSpec(memory_space=pltpu.HBM)],
            out_specs=pl.BlockSpec(memory_space=pltpu.VMEM),
            scratch_shapes=[
                pltpu.VMEM((steps, STEP_ROWS, snps), jnp.int32),
                pltpu.SemaphoreType.DMA((steps,)),
            ],
            compiler_params=pltpu.CompilerParams(vmem_limit_bytes=2 * VMEM_BYTES),
            cost_estimate=pl.CostEstimate(
                flops=half * snps, bytes_accessed=half * snps * 6, transcendentals=0
            ),
            name="convert",
        )(genotypes)

    (stats,) = call(
        functools.partial(stats_kernel, 2.0 * samples_all), ((8, snps),), allele_counts, name="stats"
    )
    both = jnp.concatenate([residual, direction], axis=0)
    upper = converted(0)
    quarter = jnp.concatenate([both] + others(both, "x"), axis=1)
    quarter, upper = lax.optimization_barrier((quarter, upper))
    lower = converted(1)
    pieces = [quarter] + others(quarter, "z")
    pieces[1], lower = lax.optimization_barrier((pieces[1], lower))
    r, d, sums = call(
        first_forward_kernel, (vec, vec, short), *pieces, upper, lower, stats,
        name="first_forward", flops=flops,
    )
    turned = [
        call(turn_kernel, ((snps, half),), part, name="turn", dtypes=(BF16,), flops=2**30)[0]
        for part in (upper, lower)
    ]

    def over_samp(v):
        return sum_over(v + from_next(v, "c", 1), "y")

    def over_snp(v):
        return sum_over(sum_over(v, "x"), "z")

    moved = None
    for iteration in range(ITERS):
        sums = over_samp(sums)
        if iteration == 0:
            u, scalars, sums = call(
                first_backward_kernel, (row, col, full), sums, *turned, stats,
                name="first_backward", flops=flops,
            )
        else:
            u, d, scalars, sums = call(
                backward_kernel, (row, vec, col, full), sums, u, r, d, scalars, *turned, stats,
                name="backward", flops=flops,
            )
        sums = over_snp(sums)
        if iteration < ITERS - 1:
            state = (sums, ridge, scalars, r, d) + (() if moved is None else (moved,))
            r, moved, sums = call(
                functools.partial(forward_kernel, float(snps_all), moved is None),
                (vec, vec, short), *state, upper, lower, stats, name="forward", flops=flops,
            )
    r, moved, norm = call(
        functools.partial(last_kernel, float(snps_all)), (vec, vec, col),
        sums, ridge, scalars, r, d, moved, name="last",
    )
    solution, r_own, d, r = call(
        own_kernel, (mine, mine, mine, mine), r, d, moved, solution, name="own", flops=2**20
    )
    norm = over_samp(norm)
    return (solution, r_own, r + (norm[:, 0:1] / scalars[:, 0:1]) * d)


def solution(mesh):
    parts = jax.sharding.Mesh(mesh.devices.reshape(4, 2, 4, 4), ("y", "c", "z", "x"))
    vec = P(None, ("y", "c", "z", "x"))
    in_specs = (P(("y", "c"), ("z", "x")), P(("z", "x")), P(), vec, vec, vec)
    return jax.shard_map(
        local, mesh=parts, in_specs=in_specs, out_specs=(vec, vec, vec), check_vma=False
    )
```

profile of v0, /device:TPU:1, one launch (start us, length us, event | category | flops | bytes accessed | tf_op | source)
XLA Modules:
  0.0 108.9 jit_solution(360068678544186777)
XLA Ops:
  1.4 2.1 %collective-permute-start.2 = (f32[8,192]{1,0:T(8,128)S(1)}, f32[8,192]{1,0:T(8,128)S(1)}, u32[]{:S(2)}, u32[]{:S(2)}) collective-permute-start(f32[8,192]{1,0:T(8,128)S(1)} %pad_maximum_fusion.1), channel_id=1, source_target_pairs={{3,0},{0,1},{1,2},{2,3},{7,4},{4,5},{5,6},{6,7},{11,8},{8,9},{9,10... | collective-permute-start | bytes 18440 | tf_op jit(solution)/shard_map/ppermute | solution.py:183
  3.5 2.5 %collective-permute-start.1 = (f32[8,192]{1,0:T(8,128)S(1)}, f32[8,192]{1,0:T(8,128)S(1)}, u32[]{:S(2)}, u32[]{:S(2)}) collective-permute-start(f32[8,192]{1,0:T(8,128)S(1)} %pad_maximum_fusion.1), channel_id=1, source_target_pairs={{2,0},{3,1},{0,2},{1,3},{6,4},{7,5},{4,6},{5,7},{10,8},{11,9},{8,1... | collective-permute-start | bytes 18440 | tf_op jit(solution)/shard_map/ppermute | solution.py:183
  7.1 3.6 %convert.2.upper.dosage.refs_5_.refs_6_ = bf16[1536,1408]{1,0:T(8,128)(2,1)S(1)} custom-call(s32[3072,1408]{1,0:T(8,128)} %genotypes.3), custom_call_target="tpu_custom_call" | custom-call | flops 2162688 | bytes 12976128 | tf_op jit(solution)/shard_map/convert/pallas_call | solution.py:211
  10.9 3.8 %collective-permute-start.3 = (f32[8,768]{1,0:T(8,128)S(1)}, f32[8,768]{1,0:T(8,128)S(1)}, u32[]{:S(2)}, u32[]{:S(2)}) collective-permute-start(f32[8,768]{1,0:T(8,128)S(1)} %pad_maximum_fusion.own), channel_id=1, source_target_pairs={{4,0},{8,4},{12,8},{0,12},{5,1},{9,5},{13,9},{1,13},{6,2},{10,6},{... | collective-permute-start | bytes 73736 | tf_op jit(solution)/shard_map/ppermute | solution.py:183
  15.9 3.6 %convert.3.lower.dosage.refs_6_.refs_7_ = bf16[1536,1408]{1,0:T(8,128)(2,1)S(1)} custom-call(s32[3072,1408]{1,0:T(8,128)} %genotypes.3), custom_call_target="tpu_custom_call" | custom-call | flops 2162688 | bytes 12976128 | tf_op jit(solution)/shard_map/convert/pallas_call | solution.py:211
  21.0 2.4 %collective-permute-start.6 = (f32[4,1536]{1,0:T(4,128)S(1)}, f32[4,1536]{1,0:T(4,128)S(1)}, u32[]{:S(2)}, u32[]{:S(2)}) collective-permute-start(f32[4,1536]{1,0:T(4,128)S(1)} %get-tuple-element.37), channel_id=1, source_target_pairs={{16,0},{0,16},{17,1},{1,17},{18,2},{2,18},{19,3},{3,19},{20,4},{4,... | collective-permute-start | bytes 73736 | tf_op jit(solution)/shard_map/ppermute | solution.py:183
  24.6 3.0 %collective-permute-start.9 = (f32[4,1536]{1,0:T(4,128)S(1)}, f32[4,1536]{1,0:T(4,128)S(1)}, u32[]{:S(2)}, u32[]{:S(2)}) collective-permute-start(f32[4,1536]{1,0:T(4,128)S(1)} %add.105), channel_id=1, source_target_pairs={{0,64},{32,96},{64,0},{96,32},{1,65},{33,97},{65,1},{97,33},{2,66}... | collective-permute-start | bytes 73736 | tf_op jit(solution)/shard_map/ppermute | solution.py:192
  29.5 1.9 %collective-permute-done.8 = f32[4,1536]{1,0:T(4,128)S(1)} collective-permute-done((f32[4,1536]{1,0:T(4,128)S(1)}, f32[4,1536]{1,0:T(4,128)S(1)}, u32[]{:S(2)}, u32[]{:S(2)}) %collective-permute-start.8) | collective-permute-done | bytes 24608 | tf_op jit(solution)/shard_map/ppermute | solution.py:192
  33.0 2.5 %collective-permute-start.11 = (f32[4,3200]{1,0:T(4,128)S(1)}, f32[4,3200]{1,0:T(4,128)S(1)}, u32[]{:S(2)}, u32[]{:S(2)}) collective-permute-start(f32[4,3200]{1,0:T(4,128)S(1)} %get-tuple-element.38), channel_id=1, source_target_pairs={{0,3},{1,2},{2,1},{3,0},{4,7},{5,6},{6,5},{7,4},{8,11},{9,10},{10,... | collective-permute-start | bytes 153608 | tf_op jit(solution)/shard_map/ppermute | solution.py:192
  35.5 1.9 %collective-permute-done.12 = f32[4,3200]{1,0:T(4,128)S(1)} collective-permute-done((f32[4,3200]{1,0:T(4,128)S(1)}, f32[4,3200]{1,0:T(4,128)S(1)}, u32[]{:S(2)}, u32[]{:S(2)}) %collective-permute-start.12) | collective-permute-done | bytes 51232 | tf_op jit(solution)/shard_map/ppermute | solution.py:192
  40.2 3.0 %collective-permute-start.14 = (f32[4,3200]{1,0:T(4,128)S(1)}, f32[4,3200]{1,0:T(4,128)S(1)}, u32[]{:S(2)}, u32[]{:S(2)}) collective-permute-start(f32[4,3200]{1,0:T(4,128)S(1)} %add_add_fusion.5), channel_id=1, source_target_pairs={{0,12},{4,8},{8,4},{12,0},{1,13},{5,9},{9,5},{13,1},{2,14},{6,10},... | collective-permute-start | bytes 153608 | tf_op jit(solution)/shard_map/ppermute | solution.py:192
  44.7 1.8 %collective-permute-done.13 = f32[4,3200]{1,0:T(4,128)S(1)} collective-permute-done((f32[4,3200]{1,0:T(4,128)S(1)}, f32[4,3200]{1,0:T(4,128)S(1)}, u32[]{:S(2)}, u32[]{:S(2)}) %collective-permute-start.13) | collective-permute-done | bytes 51232 | tf_op jit(solution)/shard_map/ppermute | solution.py:192
  47.9 4.4 %collective-permute-start.16 = (f32[4,1536]{1,0:T(4,128)S(1)}, f32[4,1536]{1,0:T(4,128)S(1)}, u32[]{:S(2)}, u32[]{:S(2)}) collective-permute-start(f32[4,1536]{1,0:T(4,128)S(1)} %get-tuple-element.42), channel_id=1, source_target_pairs={{16,0},{0,16},{17,1},{1,17},{18,2},{2,18},{19,3},{3,19},{20,4},{4,... | collective-permute-start | bytes 73736 | tf_op jit(solution)/shard_map/ppermute | solution.py:183
  60.5 1.8 %collective-permute-start.21 = (f32[4,3200]{1,0:T(4,128)S(1)}, f32[4,3200]{1,0:T(4,128)S(1)}, u32[]{:S(2)}, u32[]{:S(2)}) collective-permute-start(f32[4,3200]{1,0:T(4,128)S(1)} %get-tuple-element.45), channel_id=1, source_target_pairs={{0,3},{1,2},{2,1},{3,0},{4,7},{5,6},{6,5},{7,4},{8,11},{9,10},{10,... | collective-permute-start | bytes 153608 | tf_op jit(solution)/shard_map/ppermute | solution.py:192
  62.5 1.8 %collective-permute-done.22 = f32[4,3200]{1,0:T(4,128)S(1)} collective-permute-done((f32[4,3200]{1,0:T(4,128)S(1)}, f32[4,3200]{1,0:T(4,128)S(1)}, u32[]{:S(2)}, u32[]{:S(2)}) %collective-permute-start.22) | collective-permute-done | bytes 51232 | tf_op jit(solution)/shard_map/ppermute | solution.py:192
  68.6 1.8 %collective-permute-done.25 = f32[4,3200]{1,0:T(4,128)S(1)} collective-permute-done((f32[4,3200]{1,0:T(4,128)S(1)}, f32[4,3200]{1,0:T(4,128)S(1)}, u32[]{:S(2)}, u32[]{:S(2)}) %collective-permute-start.25) | collective-permute-done | bytes 51232 | tf_op jit(solution)/shard_map/ppermute | solution.py:192
  72.4 4.5 %collective-permute-start.26 = (f32[4,1536]{1,0:T(4,128)S(1)}, f32[4,1536]{1,0:T(4,128)S(1)}, u32[]{:S(2)}, u32[]{:S(2)}) collective-permute-start(f32[4,1536]{1,0:T(4,128)S(1)} %get-tuple-element.49), channel_id=1, source_target_pairs={{16,0},{0,16},{17,1},{1,17},{18,2},{2,18},{19,3},{3,19},{20,4},{4,... | collective-permute-start | bytes 73736 | tf_op jit(solution)/shard_map/ppermute | solution.py:183
  77.8 2.0 %collective-permute-start.29 = (f32[4,1536]{1,0:T(4,128)S(1)}, f32[4,1536]{1,0:T(4,128)S(1)}, u32[]{:S(2)}, u32[]{:S(2)}) collective-permute-start(f32[4,1536]{1,0:T(4,128)S(1)} %add.125), channel_id=1, source_target_pairs={{0,64},{32,96},{64,0},{96,32},{1,65},{33,97},{65,1},{97,33},{2,66}... | collective-permute-start | bytes 73736 | tf_op jit(solution)/shard_map/ppermute | solution.py:192
  82.0 1.6 %collective-permute-done.28 = f32[4,1536]{1,0:T(4,128)S(1)} collective-permute-done((f32[4,1536]{1,0:T(4,128)S(1)}, f32[4,1536]{1,0:T(4,128)S(1)}, u32[]{:S(2)}, u32[]{:S(2)}) %collective-permute-start.28) | collective-permute-done | bytes 24608 | tf_op jit(solution)/shard_map/ppermute | solution.py:192
  86.1 1.7 %collective-permute-start.31 = (f32[4,3200]{1,0:T(4,128)S(1)}, f32[4,3200]{1,0:T(4,128)S(1)}, u32[]{:S(2)}, u32[]{:S(2)}) collective-permute-start(f32[4,3200]{1,0:T(4,128)S(1)} %get-tuple-element.52), channel_id=1, source_target_pairs={{0,3},{1,2},{2,1},{3,0},{4,7},{5,6},{6,5},{7,4},{8,11},{9,10},{10,... | collective-permute-start | bytes 153608 | tf_op jit(solution)/shard_map/ppermute | solution.py:192
  87.8 1.8 %collective-permute-done.32 = f32[4,3200]{1,0:T(4,128)S(1)} collective-permute-done((f32[4,3200]{1,0:T(4,128)S(1)}, f32[4,3200]{1,0:T(4,128)S(1)}, u32[]{:S(2)}, u32[]{:S(2)}) %collective-permute-start.32) | collective-permute-done | bytes 51232 | tf_op jit(solution)/shard_map/ppermute | solution.py:192
  92.2 1.7 %collective-permute-start.34 = (f32[4,3200]{1,0:T(4,128)S(1)}, f32[4,3200]{1,0:T(4,128)S(1)}, u32[]{:S(2)}, u32[]{:S(2)}) collective-permute-start(f32[4,3200]{1,0:T(4,128)S(1)} %add_add_fusion.1), channel_id=1, source_target_pairs={{0,12},{4,8},{8,4},{12,0},{1,13},{5,9},{9,5},{13,1},{2,14},{6,10},... | collective-permute-start | bytes 153608 | tf_op jit(solution)/shard_map/ppermute | solution.py:192
  93.9 1.5 %collective-permute-done.35 = f32[4,3200]{1,0:T(4,128)S(1)} collective-permute-done((f32[4,3200]{1,0:T(4,128)S(1)}, f32[4,3200]{1,0:T(4,128)S(1)}, u32[]{:S(2)}, u32[]{:S(2)}) %collective-permute-start.35) | collective-permute-done | bytes 51232 | tf_op jit(solution)/shard_map/ppermute | solution.py:192
  97.2 5.1 %collective-permute-start.36 = (f32[4,128]{1,0:T(4,128)S(1)}, f32[4,128]{1,0:T(4,128)S(1)}, u32[]{:S(2)}, u32[]{:S(2)}) collective-permute-start(f32[4,128]{1,0:T(4,128)S(1)} %get-tuple-element.61), channel_id=1, source_target_pairs={{16,0},{0,16},{17,1},{1,17},{18,2},{2,18},{19,3},{3,19},{20,4},{4,... | collective-permute-start | bytes 6152 | tf_op jit(solution)/shard_map/ppermute | solution.py:183
  (98 shorter events, 46.3 us)
Async XLA Ops:
  1.4 9.3 %collective-permute-start.2 = (f32[8,192]{1,0:T(8,128)S(1)}, f32[8,192]{1,0:T(8,128)S(1)}, u32[]{:S(2)}, u32[]{:S(2)}) collective-permute-start(f32[8,192]{1,0:T(8,128)S(1)} %pad_maximum_fusion.1), channel_id=1, source_target_pairs={{3,0},{0,1},{1,2},{2,3},{7,4},{4,5},{5,6},{6,7},{11,8},{8,9},{9,10... | collective-permute-start | bytes 18440 | tf_op jit(solution)/shard_map/ppermute | solution.py:183
  3.5 7.3 %collective-permute-start.1 = (f32[8,192]{1,0:T(8,128)S(1)}, f32[8,192]{1,0:T(8,128)S(1)}, u32[]{:S(2)}, u32[]{:S(2)}) collective-permute-start(f32[8,192]{1,0:T(8,128)S(1)} %pad_maximum_fusion.1), channel_id=1, source_target_pairs={{2,0},{3,1},{0,2},{1,3},{6,4},{7,5},{4,6},{5,7},{10,8},{11,9},{8,1... | collective-permute-start | bytes 18440 | tf_op jit(solution)/shard_map/ppermute | solution.py:183
  5.9 4.8 %collective-permute-start = (f32[8,192]{1,0:T(8,128)S(1)}, f32[8,192]{1,0:T(8,128)S(1)}, u32[]{:S(2)}, u32[]{:S(2)}) collective-permute-start(f32[8,192]{1,0:T(8,128)S(1)} %pad_maximum_fusion.1), channel_id=1, source_target_pairs={{1,0},{2,1},{3,2},{0,3},{5,4},{6,5},{7,6},{4,7},{9,8},{10,9},{11,1... | collective-permute-start | bytes 18440 | tf_op jit(solution)/shard_map/ppermute | solution.py:183
  10.9 8.7 %collective-permute-start.3 = (f32[8,768]{1,0:T(8,128)S(1)}, f32[8,768]{1,0:T(8,128)S(1)}, u32[]{:S(2)}, u32[]{:S(2)}) collective-permute-start(f32[8,768]{1,0:T(8,128)S(1)} %pad_maximum_fusion.own), channel_id=1, source_target_pairs={{4,0},{8,4},{12,8},{0,12},{5,1},{9,5},{13,9},{1,13},{6,2},{10,6},{... | collective-permute-start | bytes 73736 | tf_op jit(solution)/shard_map/ppermute | solution.py:183
  14.6 5.0 %collective-permute-start.5 = (f32[8,768]{1,0:T(8,128)S(1)}, f32[8,768]{1,0:T(8,128)S(1)}, u32[]{:S(2)}, u32[]{:S(2)}) collective-permute-start(f32[8,768]{1,0:T(8,128)S(1)} %pad_maximum_fusion.own), channel_id=1, source_target_pairs={{12,0},{0,4},{4,8},{8,12},{13,1},{1,5},{5,9},{9,13},{14,2},{2,6},{... | collective-permute-start | bytes 73736 | tf_op jit(solution)/shard_map/ppermute | solution.py:183
  14.6 5.0 %collective-permute-start.4 = (f32[8,768]{1,0:T(8,128)S(1)}, f32[8,768]{1,0:T(8,128)S(1)}, u32[]{:S(2)}, u32[]{:S(2)}) collective-permute-start(f32[8,768]{1,0:T(8,128)S(1)} %pad_maximum_fusion.own), channel_id=1, source_target_pairs={{8,0},{12,4},{0,8},{4,12},{9,1},{13,5},{1,9},{5,13},{10,2},{14,6},... | collective-permute-start | bytes 73736 | tf_op jit(solution)/shard_map/ppermute | solution.py:183
  24.6 4.9 %collective-permute-start.9 = (f32[4,1536]{1,0:T(4,128)S(1)}, f32[4,1536]{1,0:T(4,128)S(1)}, u32[]{:S(2)}, u32[]{:S(2)}) collective-permute-start(f32[4,1536]{1,0:T(4,128)S(1)} %add.105), channel_id=1, source_target_pairs={{0,64},{32,96},{64,0},{96,32},{1,65},{33,97},{65,1},{97,33},{2,66}... | collective-permute-start | bytes 73736 | tf_op jit(solution)/shard_map/ppermute | solution.py:192
  32.7 4.6 %collective-permute-start.12 = (f32[4,3200]{1,0:T(4,128)S(1)}, f32[4,3200]{1,0:T(4,128)S(1)}, u32[]{:S(2)}, u32[]{:S(2)}) collective-permute-start(f32[4,3200]{1,0:T(4,128)S(1)} %get-tuple-element.38), channel_id=1, source_target_pairs={{0,2},{1,3},{2,0},{3,1},{4,6},{5,7},{6,4},{7,5},{8,10},{9,11},{10,... | collective-permute-start | bytes 153608 | tf_op jit(solution)/shard_map/ppermute | solution.py:192
  33.0 4.7 %collective-permute-start.11 = (f32[4,3200]{1,0:T(4,128)S(1)}, f32[4,3200]{1,0:T(4,128)S(1)}, u32[]{:S(2)}, u32[]{:S(2)}) collective-permute-start(f32[4,3200]{1,0:T(4,128)S(1)} %get-tuple-element.38), channel_id=1, source_target_pairs={{0,3},{1,2},{2,1},{3,0},{4,7},{5,6},{6,5},{7,4},{8,11},{9,10},{10,... | collective-permute-start | bytes 153608 | tf_op jit(solution)/shard_map/ppermute | solution.py:192
  38.8 4.5 %collective-permute-start.15 = (f32[4,3200]{1,0:T(4,128)S(1)}, f32[4,3200]{1,0:T(4,128)S(1)}, u32[]{:S(2)}, u32[]{:S(2)}) collective-permute-start(f32[4,3200]{1,0:T(4,128)S(1)} %add_add_fusion.5), channel_id=1, source_target_pairs={{0,8},{4,12},{8,0},{12,4},{1,9},{5,13},{9,1},{13,5},{2,10},{6,14},... | collective-permute-start | bytes 153608 | tf_op jit(solution)/shard_map/ppermute | solution.py:192
  40.2 4.5 %collective-permute-start.14 = (f32[4,3200]{1,0:T(4,128)S(1)}, f32[4,3200]{1,0:T(4,128)S(1)}, u32[]{:S(2)}, u32[]{:S(2)}) collective-permute-start(f32[4,3200]{1,0:T(4,128)S(1)} %add_add_fusion.5), channel_id=1, source_target_pairs={{0,12},{4,8},{8,4},{12,0},{1,13},{5,9},{9,5},{13,1},{2,14},{6,10},... | collective-permute-start | bytes 153608 | tf_op jit(solution)/shard_map/ppermute | solution.py:192
  47.9 5.2 %collective-permute-start.16 = (f32[4,1536]{1,0:T(4,128)S(1)}, f32[4,1536]{1,0:T(4,128)S(1)}, u32[]{:S(2)}, u32[]{:S(2)}) collective-permute-start(f32[4,1536]{1,0:T(4,128)S(1)} %get-tuple-element.42), channel_id=1, source_target_pairs={{16,0},{0,16},{17,1},{1,17},{18,2},{2,18},{19,3},{3,19},{20,4},{4,... | collective-permute-start | bytes 73736 | tf_op jit(solution)/shard_map/ppermute | solution.py:183
  53.1 4.3 %collective-permute-start.19 = (f32[4,1536]{1,0:T(4,128)S(1)}, f32[4,1536]{1,0:T(4,128)S(1)}, u32[]{:S(2)}, u32[]{:S(2)}) collective-permute-start(f32[4,1536]{1,0:T(4,128)S(1)} %add.115), channel_id=1, source_target_pairs={{0,64},{32,96},{64,0},{96,32},{1,65},{33,97},{65,1},{97,33},{2,66}... | collective-permute-start | bytes 73736 | tf_op jit(solution)/shard_map/ppermute | solution.py:192
  59.8 4.6 %collective-permute-start.22 = (f32[4,3200]{1,0:T(4,128)S(1)}, f32[4,3200]{1,0:T(4,128)S(1)}, u32[]{:S(2)}, u32[]{:S(2)}) collective-permute-start(f32[4,3200]{1,0:T(4,128)S(1)} %get-tuple-element.45), channel_id=1, source_target_pairs={{0,2},{1,3},{2,0},{3,1},{4,6},{5,7},{6,4},{7,5},{8,10},{9,11},{10,... | collective-permute-start | bytes 153608 | tf_op jit(solution)/shard_map/ppermute | solution.py:192
  60.5 4.5 %collective-permute-start.21 = (f32[4,3200]{1,0:T(4,128)S(1)}, f32[4,3200]{1,0:T(4,128)S(1)}, u32[]{:S(2)}, u32[]{:S(2)}) collective-permute-start(f32[4,3200]{1,0:T(4,128)S(1)} %get-tuple-element.45), channel_id=1, source_target_pairs={{0,3},{1,2},{2,1},{3,0},{4,7},{5,6},{6,5},{7,4},{8,11},{9,10},{10,... | collective-permute-start | bytes 153608 | tf_op jit(solution)/shard_map/ppermute | solution.py:192
  65.9 4.6 %collective-permute-start.25 = (f32[4,3200]{1,0:T(4,128)S(1)}, f32[4,3200]{1,0:T(4,128)S(1)}, u32[]{:S(2)}, u32[]{:S(2)}) collective-permute-start(f32[4,3200]{1,0:T(4,128)S(1)} %add_add_fusion.3), channel_id=1, source_target_pairs={{0,8},{4,12},{8,0},{12,4},{1,9},{5,13},{9,1},{13,5},{2,10},{6,14},... | collective-permute-start | bytes 153608 | tf_op jit(solution)/shard_map/ppermute | solution.py:192
  66.7 4.3 %collective-permute-start.24 = (f32[4,3200]{1,0:T(4,128)S(1)}, f32[4,3200]{1,0:T(4,128)S(1)}, u32[]{:S(2)}, u32[]{:S(2)}) collective-permute-start(f32[4,3200]{1,0:T(4,128)S(1)} %add_add_fusion.3), channel_id=1, source_target_pairs={{0,12},{4,8},{8,4},{12,0},{1,13},{5,9},{9,5},{13,1},{2,14},{6,10},... | collective-permute-start | bytes 153608 | tf_op jit(solution)/shard_map/ppermute | solution.py:192
  72.4 5.3 %collective-permute-start.26 = (f32[4,1536]{1,0:T(4,128)S(1)}, f32[4,1536]{1,0:T(4,128)S(1)}, u32[]{:S(2)}, u32[]{:S(2)}) collective-permute-start(f32[4,1536]{1,0:T(4,128)S(1)} %get-tuple-element.49), channel_id=1, source_target_pairs={{16,0},{0,16},{17,1},{1,17},{18,2},{2,18},{19,3},{3,19},{20,4},{4,... | collective-permute-start | bytes 73736 | tf_op jit(solution)/shard_map/ppermute | solution.py:183
  77.8 4.3 %collective-permute-start.29 = (f32[4,1536]{1,0:T(4,128)S(1)}, f32[4,1536]{1,0:T(4,128)S(1)}, u32[]{:S(2)}, u32[]{:S(2)}) collective-permute-start(f32[4,1536]{1,0:T(4,128)S(1)} %add.125), channel_id=1, source_target_pairs={{0,64},{32,96},{64,0},{96,32},{1,65},{33,97},{65,1},{97,33},{2,66}... | collective-permute-start | bytes 73736 | tf_op jit(solution)/shard_map/ppermute | solution.py:192
  85.0 4.5 %collective-permute-start.32 = (f32[4,3200]{1,0:T(4,128)S(1)}, f32[4,3200]{1,0:T(4,128)S(1)}, u32[]{:S(2)}, u32[]{:S(2)}) collective-permute-start(f32[4,3200]{1,0:T(4,128)S(1)} %get-tuple-element.52), channel_id=1, source_target_pairs={{0,2},{1,3},{2,0},{3,1},{4,6},{5,7},{6,4},{7,5},{8,10},{9,11},{10,... | collective-permute-start | bytes 153608 | tf_op jit(solution)/shard_map/ppermute | solution.py:192
  86.1 4.2 %collective-permute-start.31 = (f32[4,3200]{1,0:T(4,128)S(1)}, f32[4,3200]{1,0:T(4,128)S(1)}, u32[]{:S(2)}, u32[]{:S(2)}) collective-permute-start(f32[4,3200]{1,0:T(4,128)S(1)} %get-tuple-element.52), channel_id=1, source_target_pairs={{0,3},{1,2},{2,1},{3,0},{4,7},{5,6},{6,5},{7,4},{8,11},{9,10},{10,... | collective-permute-start | bytes 153608 | tf_op jit(solution)/shard_map/ppermute | solution.py:192
  90.9 4.5 %collective-permute-start.35 = (f32[4,3200]{1,0:T(4,128)S(1)}, f32[4,3200]{1,0:T(4,128)S(1)}, u32[]{:S(2)}, u32[]{:S(2)}) collective-permute-start(f32[4,3200]{1,0:T(4,128)S(1)} %add_add_fusion.1), channel_id=1, source_target_pairs={{0,8},{4,12},{8,0},{12,4},{1,9},{5,13},{9,1},{13,5},{2,10},{6,14},... | collective-permute-start | bytes 153608 | tf_op jit(solution)/shard_map/ppermute | solution.py:192
  92.2 4.2 %collective-permute-start.34 = (f32[4,3200]{1,0:T(4,128)S(1)}, f32[4,3200]{1,0:T(4,128)S(1)}, u32[]{:S(2)}, u32[]{:S(2)}) collective-permute-start(f32[4,3200]{1,0:T(4,128)S(1)} %add_add_fusion.1), channel_id=1, source_target_pairs={{0,12},{4,8},{8,4},{12,0},{1,13},{5,9},{9,5},{13,1},{2,14},{6,10},... | collective-permute-start | bytes 153608 | tf_op jit(solution)/shard_map/ppermute | solution.py:192
  97.2 5.9 %collective-permute-start.36 = (f32[4,128]{1,0:T(4,128)S(1)}, f32[4,128]{1,0:T(4,128)S(1)}, u32[]{:S(2)}, u32[]{:S(2)}) collective-permute-start(f32[4,128]{1,0:T(4,128)S(1)} %get-tuple-element.61), channel_id=1, source_target_pairs={{16,0},{0,16},{17,1},{1,17},{18,2},{2,18},{19,3},{3,19},{20,4},{4,... | collective-permute-start | bytes 6152 | tf_op jit(solution)/shard_map/ppermute | solution.py:183
  (21 other events, 124.9 us)
where the time goes:
time: 109 us
  starting transfers between devices  57.6 us (53%)
  waiting for transfers between devices  30 us (28%)
  Pallas kernels  18.5 us (17%)
  other arithmetic  1.82 us (2%)
    ppermute x30, starting transfers between devices, sum_over(): lax.ppermute(value, axis, [(i, i ^ k) for i in range(size)])  30.5 us
    ppermute x30, waiting for transfers between devices, sum_over(): lax.ppermute(value, axis, [(i, i ^ k) for i in range(size)])  27.5 us
    ppermute x10, starting transfers between devices, from_next(): return lax.ppermute(value, axis, [((i + k) % size, i) for i in range(size)])  27.1 us
    pallas_call x11, Pallas kernels, call(): pl.pallas_call(kernel, out_shape=[jax.ShapeDtypeStruct(s, t) for s, t in...  11.2 us
    pallas_call x2, Pallas kernels, converted(): pl.pallas_call(functools.partial(convert_kernel, part), out_shape=jax.Sha...  7.26 us
    ppermute x10, waiting for transfers between devices, from_next(): return lax.ppermute(value, axis, [((i + k) % size, i) for i in range(size)])  2.54 us
  transfers between devices with their start and end apart: 40, of which 28 were waited for; matrix products, arithmetic and copies ran while one was open for 0% of the time, Pallas kernels for 9%

commit v1 on v0

--- a/solution.py
+++ b/solution.py
@@ -91,12 +91,14 @@
             turned[n : n + LANES, m : m + 2 * TILE] = dosage[m : m + 2 * TILE, n : n + LANES].T
 
 
-def first_forward_kernel(own, one, two, three, upper, lower, stats, r, d, out):
+def first_forward_kernel(zero, one, two, three, upper, lower, stats, r, d, out):
     z, x = lax.axis_index("z"), lax.axis_index("x")
-    piece = own.shape[1]
-    for k, ref in enumerate((own, one, two, three)):
-        at = pl.ds(pl.multiple_of(lax.rem(z + k, 4) * piece, LANES), piece)
-        block = pltpu.roll(ref[...], x * (piece // 4), 1)
+    piece = zero.shape[1]
+    half, own = piece // 2, piece // 4
+    for k, ref in enumerate((zero, one, two, three)):
+        at = pl.ds(pl.multiple_of((z ^ k) * piece, LANES), piece)
+        pairs = [pltpu.roll(ref[:, i : i + half], (x & 1) * own, 1) for i in (0, half)]
+        block = pltpu.roll(jnp.concatenate(pairs, axis=1), (x >> 1) * half, 1)
         r[:, at] = block[0:4]
         d[:, at] = block[4:8]
     snps = upper.shape[1]
@@ -178,19 +180,28 @@
     )(*args)
 
 
-def from_next(value, axis, k):
-    size = lax.axis_size(axis)
-    return lax.ppermute(value, axis, [((i + k) % size, i) for i in range(size)])
-
-
-def others(value, axis):
-    return [from_next(value, axis, k) for k in range(1, lax.axis_size(axis))]
-
-
-def sum_over(value, axis):
-    size = lax.axis_size(axis)
-    swapped = [lax.ppermute(value, axis, [(i, i ^ k) for i in range(size)]) for k in (1, 3, 2)]
-    return (value + swapped[0]) + (swapped[1] + swapped[2])
+def swap_cores(value):
+    return lax.ppermute(value, "c", [(0, 1), (1, 0)])
+
+
+def swap_across(value, axis, k):
+    names = ("y", "c") if axis == "y" else ("c", axis)
+    size, chips = 2 * lax.axis_size(axis), lax.axis_size(axis)
+    if axis == "y":
+        pairs = [(i, i ^ (2 * k + 1)) for i in range(size)]
+    else:
+        pairs = [(i, i ^ (chips + k)) for i in range(size)]
+    return lax.ppermute(value, names, pairs)
+
+
+def crossed(value, axis):
+    one, three, two = [swap_across(value, axis, k) for k in (1, 3, 2)]
+    return [swap_cores(value), one, two, three]
+
+
+def sum_crossed(value, axis):
+    zero, one, two, three = crossed(value, axis)
+    return (zero + one) + (three + two)
 
 
 def local(genotypes, allele_counts, ridge, solution, residual, direction):
@@ -229,10 +240,10 @@
     )
     both = jnp.concatenate([residual, direction], axis=0)
     upper = converted(0)
-    quarter = jnp.concatenate([both] + others(both, "x"), axis=1)
+    quarter = jnp.concatenate(crossed(both, "x"), axis=1)
     quarter, upper = lax.optimization_barrier((quarter, upper))
     lower = converted(1)
-    pieces = [quarter] + others(quarter, "z")
+    pieces = crossed(quarter, "z")
     pieces[1], lower = lax.optimization_barrier((pieces[1], lower))
     r, d, sums = call(
         first_forward_kernel, (vec, vec, short), *pieces, upper, lower, stats,
@@ -244,10 +255,12 @@
     ]
 
     def over_samp(v):
-        return sum_over(v + from_next(v, "c", 1), "y")
+        v = v + swap_cores(v)
+        one, three, two = [swap_across(v, "y", k) for k in (1, 3, 2)]
+        return (v + one) + (three + two)
 
     def over_snp(v):
-        return sum_over(sum_over(v, "x"), "z")
+        return sum_crossed(sum_crossed(v, "x"), "z")
 
     moved = None
     for iteration in range(ITERS):

time: 109 us -> 102 us (0.936)
  starting transfers between devices: 57.6 us -> 46.6 us
  waiting for transfers between devices: 30 us -> 33.5 us
    ppermute x40 -> x48, starting transfers between devices: 57.6 us -> 46.6 us  [the longest x36 43.7 us: swap_across(): return lax.ppermute(value, names, pairs)]
    ppermute x40 -> x48, waiting for transfers between devices: 30 us -> 33.5 us  [the longest x36 30.9 us: swap_across(): return lax.ppermute(value, names, pairs)]
  transfers between devices with their start and end apart: 40 -> 48, of which waited for: 28 -> 24; matrix products, arithmetic and copies ran while one was open for 0% -> 0% of each run, Pallas kernels for 9% -> 10%
where the time goes in v1:
time: 102 us; the launch traced here: 101 us
  starting transfers between devices  46.6 us (46%)
  waiting for transfers between devices  33.5 us (33%)
  Pallas kernels  18.6 us (18%)
  other arithmetic  1.81 us (2%)
    ppermute x36, starting transfers between devices, swap_across(): return lax.ppermute(value, names, pairs)  43.7 us
    ppermute x36, waiting for transfers between devices, swap_across(): return lax.ppermute(value, names, pairs)  30.9 us
    pallas_call x11, Pallas kernels, call(): pl.pallas_call(kernel, out_shape=[jax.ShapeDtypeStruct(s, t) for s, t in...  11.3 us
    pallas_call x2, Pallas kernels, converted(): pl.pallas_call(functools.partial(convert_kernel, part), out_shape=jax.Sha...  7.26 us
    ppermute x12, starting transfers between devices, swap_cores(): return lax.ppermute(value, 'c', [(0, 1), (1, 0)])  2.87 us
    ppermute x12, waiting for transfers between devices, swap_cores(): return lax.ppermute(value, 'c', [(0, 1), (1, 0)])  2.65 us
  transfers between devices with their start and end apart: 48, of which 24 were waited for; matrix products, arithmetic and copies ran while one was open for 0% of the time, Pallas kernels for 10%

profile of v1, /device:TPU:1, one launch (start us, length us, event | category | flops | bytes accessed | tf_op | source)
XLA Modules:
  0.0 101.5 jit_solution(3731451343925694836)
XLA Ops:
  1.4 3.9 %collective-permute-start.3 = (f32[8,192]{1,0:T(8,128)S(1)}, f32[8,192]{1,0:T(8,128)S(1)}, u32[]{:S(2)}, u32[]{:S(2)}) collective-permute-start(f32[8,192]{1,0:T(8,128)S(1)} %pad_maximum_fusion.1), channel_id=1, source_target_pairs={{0,19},{1,18},{2,17},{3,16},{16,3},{17,2},{18,1},{19,0},{4,23},{5,... | collective-permute-start | bytes 18440 | tf_op jit(solution)/shard_map/ppermute | solution.py:194
  6.4 3.6 %convert.2.upper.dosage.refs_5_.refs_6_ = bf16[1536,1408]{1,0:T(8,128)(2,1)S(1)} custom-call(s32[3072,1408]{1,0:T(8,128)} %genotypes.3), custom_call_target="tpu_custom_call" | custom-call | flops 2162688 | bytes 12976128 | tf_op jit(solution)/shard_map/convert/pallas_call | solution.py:222
  10.1 2.0 %collective-permute-start.5 = (f32[8,768]{1,0:T(8,128)S(1)}, f32[8,768]{1,0:T(8,128)S(1)}, u32[]{:S(2)}, u32[]{:S(2)}) collective-permute-start(f32[8,768]{1,0:T(8,128)S(1)} %pad_maximum_fusion), channel_id=1, source_target_pairs={{0,20},{4,16},{8,28},{12,24},{16,4},{20,0},{24,12},{28,8},{1,21},{... | collective-permute-start | bytes 73736 | tf_op jit(solution)/shard_map/ppermute | solution.py:194
  12.2 2.2 %collective-permute-start.7 = (f32[8,768]{1,0:T(8,128)S(1)}, f32[8,768]{1,0:T(8,128)S(1)}, u32[]{:S(2)}, u32[]{:S(2)}) collective-permute-start(f32[8,768]{1,0:T(8,128)S(1)} %pad_maximum_fusion), channel_id=1, source_target_pairs={{0,28},{4,24},{8,20},{12,16},{16,12},{20,8},{24,4},{28,0},{1,29},{... | collective-permute-start | bytes 73736 | tf_op jit(solution)/shard_map/ppermute | solution.py:194
  15.9 3.6 %convert.3.lower.dosage.refs_6_.refs_7_ = bf16[1536,1408]{1,0:T(8,128)(2,1)S(1)} custom-call(s32[3072,1408]{1,0:T(8,128)} %genotypes.3), custom_call_target="tpu_custom_call" | custom-call | flops 2162688 | bytes 12976128 | tf_op jit(solution)/shard_map/convert/pallas_call | solution.py:222
  22.3 3.4 %collective-permute-start.11 = (f32[4,1536]{1,0:T(4,128)S(1)}, f32[4,1536]{1,0:T(4,128)S(1)}, u32[]{:S(2)}, u32[]{:S(2)}) collective-permute-start(f32[4,1536]{1,0:T(4,128)S(1)} %add.105), channel_id=1, source_target_pairs={{0,80},{16,64},{32,112},{48,96},{64,16},{80,0},{96,48},{112,32},{1... | collective-permute-start | bytes 73736 | tf_op jit(solution)/shard_map/ppermute | solution.py:194
  27.5 2.6 %collective-permute-done.10 = f32[4,1536]{1,0:T(4,128)S(1)} collective-permute-done((f32[4,1536]{1,0:T(4,128)S(1)}, f32[4,1536]{1,0:T(4,128)S(1)}, u32[]{:S(2)}, u32[]{:S(2)}) %collective-permute-start.10) | collective-permute-done | bytes 24608 | tf_op jit(solution)/shard_map/ppermute | solution.py:194
  31.4 2.7 %collective-permute-start.15 = (f32[4,3200]{1,0:T(4,128)S(1)}, f32[4,3200]{1,0:T(4,128)S(1)}, u32[]{:S(2)}, u32[]{:S(2)}) collective-permute-start(f32[4,3200]{1,0:T(4,128)S(1)} %get-tuple-element.38), channel_id=1, source_target_pairs={{0,18},{1,19},{2,16},{3,17},{16,2},{17,3},{18,0},{19,1},{4,22},{5,... | collective-permute-start | bytes 153608 | tf_op jit(solution)/shard_map/ppermute | solution.py:194
  36.4 2.8 %collective-permute-done.14 = f32[4,3200]{1,0:T(4,128)S(1)} collective-permute-done((f32[4,3200]{1,0:T(4,128)S(1)}, f32[4,3200]{1,0:T(4,128)S(1)}, u32[]{:S(2)}, u32[]{:S(2)}) %collective-permute-start.14) | collective-permute-done | bytes 51232 | tf_op jit(solution)/shard_map/ppermute | solution.py:194
  39.3 2.2 %collective-permute-start.19 = (f32[4,3200]{1,0:T(4,128)S(1)}, f32[4,3200]{1,0:T(4,128)S(1)}, u32[]{:S(2)}, u32[]{:S(2)}) collective-permute-start(f32[4,3200]{1,0:T(4,128)S(1)} %add_add_fusion.5), channel_id=1, source_target_pairs={{0,24},{4,28},{8,16},{12,20},{16,8},{20,12},{24,0},{28,4},{1,25},{... | collective-permute-start | bytes 153608 | tf_op jit(solution)/shard_map/ppermute | solution.py:194
  42.7 2.0 %collective-permute-done.19 = f32[4,3200]{1,0:T(4,128)S(1)} collective-permute-done((f32[4,3200]{1,0:T(4,128)S(1)}, f32[4,3200]{1,0:T(4,128)S(1)}, u32[]{:S(2)}, u32[]{:S(2)}) %collective-permute-start.19) | collective-permute-done | bytes 51232 | tf_op jit(solution)/shard_map/ppermute | solution.py:194
  44.6 1.6 %collective-permute-done.18 = f32[4,3200]{1,0:T(4,128)S(1)} collective-permute-done((f32[4,3200]{1,0:T(4,128)S(1)}, f32[4,3200]{1,0:T(4,128)S(1)}, u32[]{:S(2)}, u32[]{:S(2)}) %collective-permute-start.18) | collective-permute-done | bytes 51232 | tf_op jit(solution)/shard_map/ppermute | solution.py:194
  52.2 1.7 %collective-permute-done.23 = f32[4,1536]{1,0:T(4,128)S(1)} collective-permute-done((f32[4,1536]{1,0:T(4,128)S(1)}, f32[4,1536]{1,0:T(4,128)S(1)}, u32[]{:S(2)}, u32[]{:S(2)}) %collective-permute-start.23) | collective-permute-done | bytes 24608 | tf_op jit(solution)/shard_map/ppermute | solution.py:194
  57.6 1.6 %collective-permute-start.26 = (f32[4,3200]{1,0:T(4,128)S(1)}, f32[4,3200]{1,0:T(4,128)S(1)}, u32[]{:S(2)}, u32[]{:S(2)}) collective-permute-start(f32[4,3200]{1,0:T(4,128)S(1)} %get-tuple-element.45), channel_id=1, source_target_pairs={{0,19},{1,18},{2,17},{3,16},{16,3},{17,2},{18,1},{19,0},{4,23},{5,... | collective-permute-start | bytes 153608 | tf_op jit(solution)/shard_map/ppermute | solution.py:194
  59.7 1.8 %collective-permute-done.27 = f32[4,3200]{1,0:T(4,128)S(1)} collective-permute-done((f32[4,3200]{1,0:T(4,128)S(1)}, f32[4,3200]{1,0:T(4,128)S(1)}, u32[]{:S(2)}, u32[]{:S(2)}) %collective-permute-start.27) | collective-permute-done | bytes 51232 | tf_op jit(solution)/shard_map/ppermute | solution.py:194
  62.8 1.8 %collective-permute-start.31 = (f32[4,3200]{1,0:T(4,128)S(1)}, f32[4,3200]{1,0:T(4,128)S(1)}, u32[]{:S(2)}, u32[]{:S(2)}) collective-permute-start(f32[4,3200]{1,0:T(4,128)S(1)} %add_add_fusion.3), channel_id=1, source_target_pairs={{0,24},{4,28},{8,16},{12,20},{16,8},{20,12},{24,0},{28,4},{1,25},{... | collective-permute-start | bytes 153608 | tf_op jit(solution)/shard_map/ppermute | solution.py:194
  66.2 1.8 %collective-permute-done.31 = f32[4,3200]{1,0:T(4,128)S(1)} collective-permute-done((f32[4,3200]{1,0:T(4,128)S(1)}, f32[4,3200]{1,0:T(4,128)S(1)}, u32[]{:S(2)}, u32[]{:S(2)}) %collective-permute-start.31) | collective-permute-done | bytes 51232 | tf_op jit(solution)/shard_map/ppermute | solution.py:194
  72.2 2.0 %collective-permute-start.35 = (f32[4,1536]{1,0:T(4,128)S(1)}, f32[4,1536]{1,0:T(4,128)S(1)}, u32[]{:S(2)}, u32[]{:S(2)}) collective-permute-start(f32[4,1536]{1,0:T(4,128)S(1)} %add.125), channel_id=1, source_target_pairs={{0,80},{16,64},{32,112},{48,96},{64,16},{80,0},{96,48},{112,32},{1... | collective-permute-start | bytes 73736 | tf_op jit(solution)/shard_map/ppermute | solution.py:194
  75.5 1.6 %collective-permute-done.35 = f32[4,1536]{1,0:T(4,128)S(1)} collective-permute-done((f32[4,1536]{1,0:T(4,128)S(1)}, f32[4,1536]{1,0:T(4,128)S(1)}, u32[]{:S(2)}, u32[]{:S(2)}) %collective-permute-start.35) | collective-permute-done | bytes 24608 | tf_op jit(solution)/shard_map/ppermute | solution.py:194
  77.0 1.7 %collective-permute-done.34 = f32[4,1536]{1,0:T(4,128)S(1)} collective-permute-done((f32[4,1536]{1,0:T(4,128)S(1)}, f32[4,1536]{1,0:T(4,128)S(1)}, u32[]{:S(2)}, u32[]{:S(2)}) %collective-permute-start.34) | collective-permute-done | bytes 24608 | tf_op jit(solution)/shard_map/ppermute | solution.py:194
  80.1 1.9 %collective-permute-start.39 = (f32[4,3200]{1,0:T(4,128)S(1)}, f32[4,3200]{1,0:T(4,128)S(1)}, u32[]{:S(2)}, u32[]{:S(2)}) collective-permute-start(f32[4,3200]{1,0:T(4,128)S(1)} %get-tuple-element.52), channel_id=1, source_target_pairs={{0,18},{1,19},{2,16},{3,17},{16,2},{17,3},{18,0},{19,1},{4,22},{5,... | collective-permute-start | bytes 153608 | tf_op jit(solution)/shard_map/ppermute | solution.py:194
  83.5 1.9 %collective-permute-done.39 = f32[4,3200]{1,0:T(4,128)S(1)} collective-permute-done((f32[4,3200]{1,0:T(4,128)S(1)}, f32[4,3200]{1,0:T(4,128)S(1)}, u32[]{:S(2)}, u32[]{:S(2)}) %collective-permute-start.39) | collective-permute-done | bytes 51232 | tf_op jit(solution)/shard_map/ppermute | solution.py:194
  86.9 1.7 %collective-permute-start.43 = (f32[4,3200]{1,0:T(4,128)S(1)}, f32[4,3200]{1,0:T(4,128)S(1)}, u32[]{:S(2)}, u32[]{:S(2)}) collective-permute-start(f32[4,3200]{1,0:T(4,128)S(1)} %add_add_fusion.1), channel_id=1, source_target_pairs={{0,24},{4,28},{8,16},{12,20},{16,8},{20,12},{24,0},{28,4},{1,25},{... | collective-permute-start | bytes 153608 | tf_op jit(solution)/shard_map/ppermute | solution.py:194
  90.3 1.9 %collective-permute-done.43 = f32[4,3200]{1,0:T(4,128)S(1)} collective-permute-done((f32[4,3200]{1,0:T(4,128)S(1)}, f32[4,3200]{1,0:T(4,128)S(1)}, u32[]{:S(2)}, u32[]{:S(2)}) %collective-permute-start.43) | collective-permute-done | bytes 51232 | tf_op jit(solution)/shard_map/ppermute | solution.py:194
  (110 shorter events, 46.6 us)
Async XLA Ops:
  1.4 8.7 %collective-permute-start.3 = (f32[8,192]{1,0:T(8,128)S(1)}, f32[8,192]{1,0:T(8,128)S(1)}, u32[]{:S(2)}, u32[]{:S(2)}) collective-permute-start(f32[8,192]{1,0:T(8,128)S(1)} %pad_maximum_fusion.1), channel_id=1, source_target_pairs={{0,19},{1,18},{2,17},{3,16},{16,3},{17,2},{18,1},{19,0},{4,23},{5,... | collective-permute-start | bytes 18440 | tf_op jit(solution)/shard_map/ppermute | solution.py:194
  5.3 4.7 %collective-permute-start.2 = (f32[8,192]{1,0:T(8,128)S(1)}, f32[8,192]{1,0:T(8,128)S(1)}, u32[]{:S(2)}, u32[]{:S(2)}) collective-permute-start(f32[8,192]{1,0:T(8,128)S(1)} %pad_maximum_fusion.1), channel_id=1, source_target_pairs={{0,18},{1,19},{2,16},{3,17},{16,2},{17,3},{18,0},{19,1},{4,22},{5,... | collective-permute-start | bytes 18440 | tf_op jit(solution)/shard_map/ppermute | solution.py:194
  10.1 9.4 %collective-permute-start.5 = (f32[8,768]{1,0:T(8,128)S(1)}, f32[8,768]{1,0:T(8,128)S(1)}, u32[]{:S(2)}, u32[]{:S(2)}) collective-permute-start(f32[8,768]{1,0:T(8,128)S(1)} %pad_maximum_fusion), channel_id=1, source_target_pairs={{0,20},{4,16},{8,28},{12,24},{16,4},{20,0},{24,12},{28,8},{1,21},{... | collective-permute-start | bytes 73736 | tf_op jit(solution)/shard_map/ppermute | solution.py:194
  12.2 7.4 %collective-permute-start.7 = (f32[8,768]{1,0:T(8,128)S(1)}, f32[8,768]{1,0:T(8,128)S(1)}, u32[]{:S(2)}, u32[]{:S(2)}) collective-permute-start(f32[8,768]{1,0:T(8,128)S(1)} %pad_maximum_fusion), channel_id=1, source_target_pairs={{0,28},{4,24},{8,20},{12,16},{16,12},{20,8},{24,4},{28,0},{1,29},{... | collective-permute-start | bytes 73736 | tf_op jit(solution)/shard_map/ppermute | solution.py:194
  14.4 5.2 %collective-permute-start.6 = (f32[8,768]{1,0:T(8,128)S(1)}, f32[8,768]{1,0:T(8,128)S(1)}, u32[]{:S(2)}, u32[]{:S(2)}) collective-permute-start(f32[8,768]{1,0:T(8,128)S(1)} %pad_maximum_fusion), channel_id=1, source_target_pairs={{0,24},{4,28},{8,16},{12,20},{16,8},{20,12},{24,0},{28,4},{1,25},{... | collective-permute-start | bytes 73736 | tf_op jit(solution)/shard_map/ppermute | solution.py:194
  22.3 5.2 %collective-permute-start.11 = (f32[4,1536]{1,0:T(4,128)S(1)}, f32[4,1536]{1,0:T(4,128)S(1)}, u32[]{:S(2)}, u32[]{:S(2)}) collective-permute-start(f32[4,1536]{1,0:T(4,128)S(1)} %add.105), channel_id=1, source_target_pairs={{0,80},{16,64},{32,112},{48,96},{64,16},{80,0},{96,48},{112,32},{1... | collective-permute-start | bytes 73736 | tf_op jit(solution)/shard_map/ppermute | solution.py:194
  25.6 4.5 %collective-permute-start.10 = (f32[4,1536]{1,0:T(4,128)S(1)}, f32[4,1536]{1,0:T(4,128)S(1)}, u32[]{:S(2)}, u32[]{:S(2)}) collective-permute-start(f32[4,1536]{1,0:T(4,128)S(1)} %add.105), channel_id=1, source_target_pairs={{0,112},{16,96},{32,80},{48,64},{64,48},{80,32},{96,16},{112,0},{1... | collective-permute-start | bytes 73736 | tf_op jit(solution)/shard_map/ppermute | solution.py:194
  31.4 5.1 %collective-permute-start.15 = (f32[4,3200]{1,0:T(4,128)S(1)}, f32[4,3200]{1,0:T(4,128)S(1)}, u32[]{:S(2)}, u32[]{:S(2)}) collective-permute-start(f32[4,3200]{1,0:T(4,128)S(1)} %get-tuple-element.38), channel_id=1, source_target_pairs={{0,18},{1,19},{2,16},{3,17},{16,2},{17,3},{18,0},{19,1},{4,22},{5,... | collective-permute-start | bytes 153608 | tf_op jit(solution)/shard_map/ppermute | solution.py:194
  34.0 5.2 %collective-permute-start.14 = (f32[4,3200]{1,0:T(4,128)S(1)}, f32[4,3200]{1,0:T(4,128)S(1)}, u32[]{:S(2)}, u32[]{:S(2)}) collective-permute-start(f32[4,3200]{1,0:T(4,128)S(1)} %get-tuple-element.38), channel_id=1, source_target_pairs={{0,19},{1,18},{2,17},{3,16},{16,3},{17,2},{18,1},{19,0},{4,23},{5,... | collective-permute-start | bytes 153608 | tf_op jit(solution)/shard_map/ppermute | solution.py:194
  39.3 5.4 %collective-permute-start.19 = (f32[4,3200]{1,0:T(4,128)S(1)}, f32[4,3200]{1,0:T(4,128)S(1)}, u32[]{:S(2)}, u32[]{:S(2)}) collective-permute-start(f32[4,3200]{1,0:T(4,128)S(1)} %add_add_fusion.5), channel_id=1, source_target_pairs={{0,24},{4,28},{8,16},{12,20},{16,8},{20,12},{24,0},{28,4},{1,25},{... | collective-permute-start | bytes 153608 | tf_op jit(solution)/shard_map/ppermute | solution.py:194
  41.5 4.8 %collective-permute-start.18 = (f32[4,3200]{1,0:T(4,128)S(1)}, f32[4,3200]{1,0:T(4,128)S(1)}, u32[]{:S(2)}, u32[]{:S(2)}) collective-permute-start(f32[4,3200]{1,0:T(4,128)S(1)} %add_add_fusion.5), channel_id=1, source_target_pairs={{0,28},{4,24},{8,20},{12,16},{16,12},{20,8},{24,4},{28,0},{1,29},{... | collective-permute-start | bytes 153608 | tf_op jit(solution)/shard_map/ppermute | solution.py:194
  49.0 4.8 %collective-permute-start.23 = (f32[4,1536]{1,0:T(4,128)S(1)}, f32[4,1536]{1,0:T(4,128)S(1)}, u32[]{:S(2)}, u32[]{:S(2)}) collective-permute-start(f32[4,1536]{1,0:T(4,128)S(1)} %add.115), channel_id=1, source_target_pairs={{0,80},{16,64},{32,112},{48,96},{64,16},{80,0},{96,48},{112,32},{1... | collective-permute-start | bytes 73736 | tf_op jit(solution)/shard_map/ppermute | solution.py:194
  50.5 4.5 %collective-permute-start.22 = (f32[4,1536]{1,0:T(4,128)S(1)}, f32[4,1536]{1,0:T(4,128)S(1)}, u32[]{:S(2)}, u32[]{:S(2)}) collective-permute-start(f32[4,1536]{1,0:T(4,128)S(1)} %add.115), channel_id=1, source_target_pairs={{0,112},{16,96},{32,80},{48,64},{64,48},{80,32},{96,16},{112,0},{1... | collective-permute-start | bytes 73736 | tf_op jit(solution)/shard_map/ppermute | solution.py:194
  56.2 5.2 %collective-permute-start.27 = (f32[4,3200]{1,0:T(4,128)S(1)}, f32[4,3200]{1,0:T(4,128)S(1)}, u32[]{:S(2)}, u32[]{:S(2)}) collective-permute-start(f32[4,3200]{1,0:T(4,128)S(1)} %get-tuple-element.45), channel_id=1, source_target_pairs={{0,18},{1,19},{2,16},{3,17},{16,2},{17,3},{18,0},{19,1},{4,22},{5,... | collective-permute-start | bytes 153608 | tf_op jit(solution)/shard_map/ppermute | solution.py:194
  57.6 5.0 %collective-permute-start.26 = (f32[4,3200]{1,0:T(4,128)S(1)}, f32[4,3200]{1,0:T(4,128)S(1)}, u32[]{:S(2)}, u32[]{:S(2)}) collective-permute-start(f32[4,3200]{1,0:T(4,128)S(1)} %get-tuple-element.45), channel_id=1, source_target_pairs={{0,19},{1,18},{2,17},{3,16},{16,3},{17,2},{18,1},{19,0},{4,23},{5,... | collective-permute-start | bytes 153608 | tf_op jit(solution)/shard_map/ppermute | solution.py:194
  62.8 5.2 %collective-permute-start.31 = (f32[4,3200]{1,0:T(4,128)S(1)}, f32[4,3200]{1,0:T(4,128)S(1)}, u32[]{:S(2)}, u32[]{:S(2)}) collective-permute-start(f32[4,3200]{1,0:T(4,128)S(1)} %add_add_fusion.3), channel_id=1, source_target_pairs={{0,24},{4,28},{8,16},{12,20},{16,8},{20,12},{24,0},{28,4},{1,25},{... | collective-permute-start | bytes 153608 | tf_op jit(solution)/shard_map/ppermute | solution.py:194
  64.6 4.9 %collective-permute-start.30 = (f32[4,3200]{1,0:T(4,128)S(1)}, f32[4,3200]{1,0:T(4,128)S(1)}, u32[]{:S(2)}, u32[]{:S(2)}) collective-permute-start(f32[4,3200]{1,0:T(4,128)S(1)} %add_add_fusion.3), channel_id=1, source_target_pairs={{0,28},{4,24},{8,20},{12,16},{16,12},{20,8},{24,4},{28,0},{1,29},{... | collective-permute-start | bytes 153608 | tf_op jit(solution)/shard_map/ppermute | solution.py:194
  72.2 4.8 %collective-permute-start.35 = (f32[4,1536]{1,0:T(4,128)S(1)}, f32[4,1536]{1,0:T(4,128)S(1)}, u32[]{:S(2)}, u32[]{:S(2)}) collective-permute-start(f32[4,1536]{1,0:T(4,128)S(1)} %add.125), channel_id=1, source_target_pairs={{0,80},{16,64},{32,112},{48,96},{64,16},{80,0},{96,48},{112,32},{1... | collective-permute-start | bytes 73736 | tf_op jit(solution)/shard_map/ppermute | solution.py:194
  74.2 4.5 %collective-permute-start.34 = (f32[4,1536]{1,0:T(4,128)S(1)}, f32[4,1536]{1,0:T(4,128)S(1)}, u32[]{:S(2)}, u32[]{:S(2)}) collective-permute-start(f32[4,1536]{1,0:T(4,128)S(1)} %add.125), channel_id=1, source_target_pairs={{0,112},{16,96},{32,80},{48,64},{64,48},{80,32},{96,16},{112,0},{1... | collective-permute-start | bytes 73736 | tf_op jit(solution)/shard_map/ppermute | solution.py:194
  80.1 5.3 %collective-permute-start.39 = (f32[4,3200]{1,0:T(4,128)S(1)}, f32[4,3200]{1,0:T(4,128)S(1)}, u32[]{:S(2)}, u32[]{:S(2)}) collective-permute-start(f32[4,3200]{1,0:T(4,128)S(1)} %get-tuple-element.52), channel_id=1, source_target_pairs={{0,18},{1,19},{2,16},{3,17},{16,2},{17,3},{18,0},{19,1},{4,22},{5,... | collective-permute-start | bytes 153608 | tf_op jit(solution)/shard_map/ppermute | solution.py:194
  81.9 4.9 %collective-permute-start.38 = (f32[4,3200]{1,0:T(4,128)S(1)}, f32[4,3200]{1,0:T(4,128)S(1)}, u32[]{:S(2)}, u32[]{:S(2)}) collective-permute-start(f32[4,3200]{1,0:T(4,128)S(1)} %get-tuple-element.52), channel_id=1, source_target_pairs={{0,19},{1,18},{2,17},{3,16},{16,3},{17,2},{18,1},{19,0},{4,23},{5,... | collective-permute-start | bytes 153608 | tf_op jit(solution)/shard_map/ppermute | solution.py:194
  86.9 5.4 %collective-permute-start.43 = (f32[4,3200]{1,0:T(4,128)S(1)}, f32[4,3200]{1,0:T(4,128)S(1)}, u32[]{:S(2)}, u32[]{:S(2)}) collective-permute-start(f32[4,3200]{1,0:T(4,128)S(1)} %add_add_fusion.1), channel_id=1, source_target_pairs={{0,24},{4,28},{8,16},{12,20},{16,8},{20,12},{24,0},{28,4},{1,25},{... | collective-permute-start | bytes 153608 | tf_op jit(solution)/shard_map/ppermute | solution.py:194
  88.6 4.9 %collective-permute-start.42 = (f32[4,3200]{1,0:T(4,128)S(1)}, f32[4,3200]{1,0:T(4,128)S(1)}, u32[]{:S(2)}, u32[]{:S(2)}) collective-permute-start(f32[4,3200]{1,0:T(4,128)S(1)} %add_add_fusion.1), channel_id=1, source_target_pairs={{0,28},{4,24},{8,20},{12,16},{16,12},{20,8},{24,4},{28,0},{1,29},{... | collective-permute-start | bytes 153608 | tf_op jit(solution)/shard_map/ppermute | solution.py:194
  95.0 4.5 %collective-permute-start.47 = (f32[4,128]{1,0:T(4,128)S(1)}, f32[4,128]{1,0:T(4,128)S(1)}, u32[]{:S(2)}, u32[]{:S(2)}) collective-permute-start(f32[4,128]{1,0:T(4,128)S(1)} %add.135), channel_id=1, source_target_pairs={{0,80},{16,64},{32,112},{48,96},{64,16},{80,0},{96,48},{112,32},{1... | collective-permute-start | bytes 6152 | tf_op jit(solution)/shard_map/ppermute | solution.py:194
  (27 other events, 129.9 us)

commit v2 on v1

--- a/solution.py
+++ b/solution.py
@@ -244,7 +244,7 @@
     quarter, upper = lax.optimization_barrier((quarter, upper))
     lower = converted(1)
     pieces = crossed(quarter, "z")
-    pieces[1], lower = lax.optimization_barrier((pieces[1], lower))
+    *pieces, lower = lax.optimization_barrier((*pieces, lower))
     r, d, sums = call(
         first_forward_kernel, (vec, vec, short), *pieces, upper, lower, stats,
         name="first_forward", flops=flops,

time: 102 us -> 102 us (level)
  transfers between devices with their start and end apart: 48 -> 48, of which waited for: 24 -> 25; matrix products, arithmetic and copies ran while one was open for 0% -> 0% of each run, Pallas kernels for 10% -> 10%
where the time goes in v2:
time: 102 us; the launch traced here: 101 us
  starting transfers between devices  46.5 us (46%)
  waiting for transfers between devices  33.6 us (33%)
  Pallas kernels  18.6 us (18%)
  other arithmetic  1.81 us (2%)
    ppermute x36, starting transfers between devices, swap_across(): return lax.ppermute(value, names, pairs)  43.5 us
    ppermute x36, waiting for transfers between devices, swap_across(): return lax.ppermute(value, names, pairs)  31 us
    pallas_call x11, Pallas kernels, call(): pl.pallas_call(kernel, out_shape=[jax.ShapeDtypeStruct(s, t) for s, t in...  11.3 us
    pallas_call x2, Pallas kernels, converted(): pl.pallas_call(functools.partial(convert_kernel, part), out_shape=jax.Sha...  7.26 us
    ppermute x12, starting transfers between devices, swap_cores(): return lax.ppermute(value, 'c', [(0, 1), (1, 0)])  3.02 us
    ppermute x12, waiting for transfers between devices, swap_cores(): return lax.ppermute(value, 'c', [(0, 1), (1, 0)])  2.65 us
  transfers between devices with their start and end apart: 48, of which 25 were waited for; matrix products, arithmetic and copies ran while one was open for 0% of the time, Pallas kernels for 10%

profile of v2, /device:TPU:1, one launch (start us, length us, event | category | flops | bytes accessed | tf_op | source)
XLA Modules:
  0.0 101.5 jit_solution(8464805420812592180)
XLA Ops:
  1.4 3.9 %collective-permute-start.3 = (f32[8,192]{1,0:T(8,128)S(1)}, f32[8,192]{1,0:T(8,128)S(1)}, u32[]{:S(2)}, u32[]{:S(2)}) collective-permute-start(f32[8,192]{1,0:T(8,128)S(1)} %pad_maximum_fusion.1), channel_id=1, source_target_pairs={{0,19},{1,18},{2,17},{3,16},{16,3},{17,2},{18,1},{19,0},{4,23},{5,... | collective-permute-start | bytes 18440 | tf_op jit(solution)/shard_map/ppermute | solution.py:194
  6.4 3.6 %convert.2.upper.dosage.refs_5_.refs_6_ = bf16[1536,1408]{1,0:T(8,128)(2,1)S(1)} custom-call(s32[3072,1408]{1,0:T(8,128)} %genotypes.3), custom_call_target="tpu_custom_call" | custom-call | flops 2162688 | bytes 12976128 | tf_op jit(solution)/shard_map/convert/pallas_call | solution.py:222
  10.1 4.2 %collective-permute-start.7 = (f32[8,768]{1,0:T(8,128)S(1)}, f32[8,768]{1,0:T(8,128)S(1)}, u32[]{:S(2)}, u32[]{:S(2)}) collective-permute-start(f32[8,768]{1,0:T(8,128)S(1)} %pad_maximum_fusion), channel_id=1, source_target_pairs={{0,28},{4,24},{8,20},{12,16},{16,12},{20,8},{24,4},{28,0},{1,29},{... | collective-permute-start | bytes 73736 | tf_op jit(solution)/shard_map/ppermute | solution.py:194
  15.4 3.6 %convert.3.lower.dosage.refs_6_.refs_7_ = bf16[1536,1408]{1,0:T(8,128)(2,1)S(1)} custom-call(s32[3072,1408]{1,0:T(8,128)} %genotypes.3), custom_call_target="tpu_custom_call" | custom-call | flops 2162688 | bytes 12976128 | tf_op jit(solution)/shard_map/convert/pallas_call | solution.py:222
  21.8 3.4 %collective-permute-start.11 = (f32[4,1536]{1,0:T(4,128)S(1)}, f32[4,1536]{1,0:T(4,128)S(1)}, u32[]{:S(2)}, u32[]{:S(2)}) collective-permute-start(f32[4,1536]{1,0:T(4,128)S(1)} %add.105), channel_id=1, source_target_pairs={{0,80},{16,64},{32,112},{48,96},{64,16},{80,0},{96,48},{112,32},{1... | collective-permute-start | bytes 73736 | tf_op jit(solution)/shard_map/ppermute | solution.py:194
  27.1 2.6 %collective-permute-done.10 = f32[4,1536]{1,0:T(4,128)S(1)} collective-permute-done((f32[4,1536]{1,0:T(4,128)S(1)}, f32[4,1536]{1,0:T(4,128)S(1)}, u32[]{:S(2)}, u32[]{:S(2)}) %collective-permute-start.10) | collective-permute-done | bytes 24608 | tf_op jit(solution)/shard_map/ppermute | solution.py:194
  30.9 2.7 %collective-permute-start.15 = (f32[4,3200]{1,0:T(4,128)S(1)}, f32[4,3200]{1,0:T(4,128)S(1)}, u32[]{:S(2)}, u32[]{:S(2)}) collective-permute-start(f32[4,3200]{1,0:T(4,128)S(1)} %get-tuple-element.44), channel_id=1, source_target_pairs={{0,18},{1,19},{2,16},{3,17},{16,2},{17,3},{18,0},{19,1},{4,22},{5,... | collective-permute-start | bytes 153608 | tf_op jit(solution)/shard_map/ppermute | solution.py:194
  36.0 2.8 %collective-permute-done.14 = f32[4,3200]{1,0:T(4,128)S(1)} collective-permute-done((f32[4,3200]{1,0:T(4,128)S(1)}, f32[4,3200]{1,0:T(4,128)S(1)}, u32[]{:S(2)}, u32[]{:S(2)}) %collective-permute-start.14) | collective-permute-done | bytes 51232 | tf_op jit(solution)/shard_map/ppermute | solution.py:194
  38.8 2.7 %collective-permute-start.19 = (f32[4,3200]{1,0:T(4,128)S(1)}, f32[4,3200]{1,0:T(4,128)S(1)}, u32[]{:S(2)}, u32[]{:S(2)}) collective-permute-start(f32[4,3200]{1,0:T(4,128)S(1)} %add_add_fusion.5), channel_id=1, source_target_pairs={{0,24},{4,28},{8,16},{12,20},{16,8},{20,12},{24,0},{28,4},{1,25},{... | collective-permute-start | bytes 153608 | tf_op jit(solution)/shard_map/ppermute | solution.py:194
  42.7 1.5 %collective-permute-done.19 = f32[4,3200]{1,0:T(4,128)S(1)} collective-permute-done((f32[4,3200]{1,0:T(4,128)S(1)}, f32[4,3200]{1,0:T(4,128)S(1)}, u32[]{:S(2)}, u32[]{:S(2)}) %collective-permute-start.19) | collective-permute-done | bytes 51232 | tf_op jit(solution)/shard_map/ppermute | solution.py:194
  44.2 2.1 %collective-permute-done.18 = f32[4,3200]{1,0:T(4,128)S(1)} collective-permute-done((f32[4,3200]{1,0:T(4,128)S(1)}, f32[4,3200]{1,0:T(4,128)S(1)}, u32[]{:S(2)}, u32[]{:S(2)}) %collective-permute-start.18) | collective-permute-done | bytes 51232 | tf_op jit(solution)/shard_map/ppermute | solution.py:194
  52.2 1.7 %collective-permute-done.23 = f32[4,1536]{1,0:T(4,128)S(1)} collective-permute-done((f32[4,1536]{1,0:T(4,128)S(1)}, f32[4,1536]{1,0:T(4,128)S(1)}, u32[]{:S(2)}, u32[]{:S(2)}) %collective-permute-start.23) | collective-permute-done | bytes 24608 | tf_op jit(solution)/shard_map/ppermute | solution.py:194
  59.6 1.8 %collective-permute-done.27 = f32[4,3200]{1,0:T(4,128)S(1)} collective-permute-done((f32[4,3200]{1,0:T(4,128)S(1)}, f32[4,3200]{1,0:T(4,128)S(1)}, u32[]{:S(2)}, u32[]{:S(2)}) %collective-permute-start.27) | collective-permute-done | bytes 51232 | tf_op jit(solution)/shard_map/ppermute | solution.py:194
  62.7 1.8 %collective-permute-start.31 = (f32[4,3200]{1,0:T(4,128)S(1)}, f32[4,3200]{1,0:T(4,128)S(1)}, u32[]{:S(2)}, u32[]{:S(2)}) collective-permute-start(f32[4,3200]{1,0:T(4,128)S(1)} %add_add_fusion.3), channel_id=1, source_target_pairs={{0,24},{4,28},{8,16},{12,20},{16,8},{20,12},{24,0},{28,4},{1,25},{... | collective-permute-start | bytes 153608 | tf_op jit(solution)/shard_map/ppermute | solution.py:194
  66.1 1.9 %collective-permute-done.31 = f32[4,3200]{1,0:T(4,128)S(1)} collective-permute-done((f32[4,3200]{1,0:T(4,128)S(1)}, f32[4,3200]{1,0:T(4,128)S(1)}, u32[]{:S(2)}, u32[]{:S(2)}) %collective-permute-start.31) | collective-permute-done | bytes 51232 | tf_op jit(solution)/shard_map/ppermute | solution.py:194
  72.2 2.0 %collective-permute-start.35 = (f32[4,1536]{1,0:T(4,128)S(1)}, f32[4,1536]{1,0:T(4,128)S(1)}, u32[]{:S(2)}, u32[]{:S(2)}) collective-permute-start(f32[4,1536]{1,0:T(4,128)S(1)} %add.125), channel_id=1, source_target_pairs={{0,80},{16,64},{32,112},{48,96},{64,16},{80,0},{96,48},{112,32},{1... | collective-permute-start | bytes 73736 | tf_op jit(solution)/shard_map/ppermute | solution.py:194
  75.5 1.6 %collective-permute-done.35 = f32[4,1536]{1,0:T(4,128)S(1)} collective-permute-done((f32[4,1536]{1,0:T(4,128)S(1)}, f32[4,1536]{1,0:T(4,128)S(1)}, u32[]{:S(2)}, u32[]{:S(2)}) %collective-permute-start.35) | collective-permute-done | bytes 24608 | tf_op jit(solution)/shard_map/ppermute | solution.py:194
  77.0 1.7 %collective-permute-done.34 = f32[4,1536]{1,0:T(4,128)S(1)} collective-permute-done((f32[4,1536]{1,0:T(4,128)S(1)}, f32[4,1536]{1,0:T(4,128)S(1)}, u32[]{:S(2)}, u32[]{:S(2)}) %collective-permute-start.34) | collective-permute-done | bytes 24608 | tf_op jit(solution)/shard_map/ppermute | solution.py:194
  80.1 1.9 %collective-permute-start.39 = (f32[4,3200]{1,0:T(4,128)S(1)}, f32[4,3200]{1,0:T(4,128)S(1)}, u32[]{:S(2)}, u32[]{:S(2)}) collective-permute-start(f32[4,3200]{1,0:T(4,128)S(1)} %get-tuple-element.58), channel_id=1, source_target_pairs={{0,18},{1,19},{2,16},{3,17},{16,2},{17,3},{18,0},{19,1},{4,22},{5,... | collective-permute-start | bytes 153608 | tf_op jit(solution)/shard_map/ppermute | solution.py:194
  83.5 1.9 %collective-permute-done.39 = f32[4,3200]{1,0:T(4,128)S(1)} collective-permute-done((f32[4,3200]{1,0:T(4,128)S(1)}, f32[4,3200]{1,0:T(4,128)S(1)}, u32[]{:S(2)}, u32[]{:S(2)}) %collective-permute-start.39) | collective-permute-done | bytes 51232 | tf_op jit(solution)/shard_map/ppermute | solution.py:194
  85.4 1.4 %collective-permute-done.38 = f32[4,3200]{1,0:T(4,128)S(1)} collective-permute-done((f32[4,3200]{1,0:T(4,128)S(1)}, f32[4,3200]{1,0:T(4,128)S(1)}, u32[]{:S(2)}, u32[]{:S(2)}) %collective-permute-start.38) | collective-permute-done | bytes 51232 | tf_op jit(solution)/shard_map/ppermute | solution.py:194
  86.9 1.7 %collective-permute-start.43 = (f32[4,3200]{1,0:T(4,128)S(1)}, f32[4,3200]{1,0:T(4,128)S(1)}, u32[]{:S(2)}, u32[]{:S(2)}) collective-permute-start(f32[4,3200]{1,0:T(4,128)S(1)} %add_add_fusion.1), channel_id=1, source_target_pairs={{0,24},{4,28},{8,16},{12,20},{16,8},{20,12},{24,0},{28,4},{1,25},{... | collective-permute-start | bytes 153608 | tf_op jit(solution)/shard_map/ppermute | solution.py:194
  90.3 1.9 %collective-permute-done.43 = f32[4,3200]{1,0:T(4,128)S(1)} collective-permute-done((f32[4,3200]{1,0:T(4,128)S(1)}, f32[4,3200]{1,0:T(4,128)S(1)}, u32[]{:S(2)}, u32[]{:S(2)}) %collective-permute-start.43) | collective-permute-done | bytes 51232 | tf_op jit(solution)/shard_map/ppermute | solution.py:194
  95.0 1.4 %collective-permute-start.47 = (f32[4,128]{1,0:T(4,128)S(1)}, f32[4,128]{1,0:T(4,128)S(1)}, u32[]{:S(2)}, u32[]{:S(2)}) collective-permute-start(f32[4,128]{1,0:T(4,128)S(1)} %add.135), channel_id=1, source_target_pairs={{0,80},{16,64},{32,112},{48,96},{64,16},{80,0},{96,48},{112,32},{1... | collective-permute-start | bytes 6152 | tf_op jit(solution)/shard_map/ppermute | solution.py:194
  (110 shorter events, 44.8 us)
Async XLA Ops:
  1.4 8.7 %collective-permute-start.3 = (f32[8,192]{1,0:T(8,128)S(1)}, f32[8,192]{1,0:T(8,128)S(1)}, u32[]{:S(2)}, u32[]{:S(2)}) collective-permute-start(f32[8,192]{1,0:T(8,128)S(1)} %pad_maximum_fusion.1), channel_id=1, source_target_pairs={{0,19},{1,18},{2,17},{3,16},{16,3},{17,2},{18,1},{19,0},{4,23},{5,... | collective-permute-start | bytes 18440 | tf_op jit(solution)/shard_map/ppermute | solution.py:194
  5.3 4.7 %collective-permute-start.2 = (f32[8,192]{1,0:T(8,128)S(1)}, f32[8,192]{1,0:T(8,128)S(1)}, u32[]{:S(2)}, u32[]{:S(2)}) collective-permute-start(f32[8,192]{1,0:T(8,128)S(1)} %pad_maximum_fusion.1), channel_id=1, source_target_pairs={{0,18},{1,19},{2,16},{3,17},{16,2},{17,3},{18,0},{19,1},{4,22},{5,... | collective-permute-start | bytes 18440 | tf_op jit(solution)/shard_map/ppermute | solution.py:194
  10.1 8.9 %collective-permute-start.7 = (f32[8,768]{1,0:T(8,128)S(1)}, f32[8,768]{1,0:T(8,128)S(1)}, u32[]{:S(2)}, u32[]{:S(2)}) collective-permute-start(f32[8,768]{1,0:T(8,128)S(1)} %pad_maximum_fusion), channel_id=1, source_target_pairs={{0,28},{4,24},{8,20},{12,16},{16,12},{20,8},{24,4},{28,0},{1,29},{... | collective-permute-start | bytes 73736 | tf_op jit(solution)/shard_map/ppermute | solution.py:194
  14.3 4.8 %collective-permute-start.6 = (f32[8,768]{1,0:T(8,128)S(1)}, f32[8,768]{1,0:T(8,128)S(1)}, u32[]{:S(2)}, u32[]{:S(2)}) collective-permute-start(f32[8,768]{1,0:T(8,128)S(1)} %pad_maximum_fusion), channel_id=1, source_target_pairs={{0,24},{4,28},{8,16},{12,20},{16,8},{20,12},{24,0},{28,4},{1,25},{... | collective-permute-start | bytes 73736 | tf_op jit(solution)/shard_map/ppermute | solution.py:194
  14.3 4.8 %collective-permute-start.5 = (f32[8,768]{1,0:T(8,128)S(1)}, f32[8,768]{1,0:T(8,128)S(1)}, u32[]{:S(2)}, u32[]{:S(2)}) collective-permute-start(f32[8,768]{1,0:T(8,128)S(1)} %pad_maximum_fusion), channel_id=1, source_target_pairs={{0,20},{4,16},{8,28},{12,24},{16,4},{20,0},{24,12},{28,8},{1,21},{... | collective-permute-start | bytes 73736 | tf_op jit(solution)/shard_map/ppermute | solution.py:194
  21.8 5.2 %collective-permute-start.11 = (f32[4,1536]{1,0:T(4,128)S(1)}, f32[4,1536]{1,0:T(4,128)S(1)}, u32[]{:S(2)}, u32[]{:S(2)}) collective-permute-start(f32[4,1536]{1,0:T(4,128)S(1)} %add.105), channel_id=1, source_target_pairs={{0,80},{16,64},{32,112},{48,96},{64,16},{80,0},{96,48},{112,32},{1... | collective-permute-start | bytes 73736 | tf_op jit(solution)/shard_map/ppermute | solution.py:194
  25.2 4.5 %collective-permute-start.10 = (f32[4,1536]{1,0:T(4,128)S(1)}, f32[4,1536]{1,0:T(4,128)S(1)}, u32[]{:S(2)}, u32[]{:S(2)}) collective-permute-start(f32[4,1536]{1,0:T(4,128)S(1)} %add.105), channel_id=1, source_target_pairs={{0,112},{16,96},{32,80},{48,64},{64,48},{80,32},{96,16},{112,0},{1... | collective-permute-start | bytes 73736 | tf_op jit(solution)/shard_map/ppermute | solution.py:194
  30.9 5.1 %collective-permute-start.15 = (f32[4,3200]{1,0:T(4,128)S(1)}, f32[4,3200]{1,0:T(4,128)S(1)}, u32[]{:S(2)}, u32[]{:S(2)}) collective-permute-start(f32[4,3200]{1,0:T(4,128)S(1)} %get-tuple-element.44), channel_id=1, source_target_pairs={{0,18},{1,19},{2,16},{3,17},{16,2},{17,3},{18,0},{19,1},{4,22},{5,... | collective-permute-start | bytes 153608 | tf_op jit(solution)/shard_map/ppermute | solution.py:194
  33.6 5.2 %collective-permute-start.14 = (f32[4,3200]{1,0:T(4,128)S(1)}, f32[4,3200]{1,0:T(4,128)S(1)}, u32[]{:S(2)}, u32[]{:S(2)}) collective-permute-start(f32[4,3200]{1,0:T(4,128)S(1)} %get-tuple-element.44), channel_id=1, source_target_pairs={{0,19},{1,18},{2,17},{3,16},{16,3},{17,2},{18,1},{19,0},{4,23},{5,... | collective-permute-start | bytes 153608 | tf_op jit(solution)/shard_map/ppermute | solution.py:194
  38.8 5.4 %collective-permute-start.19 = (f32[4,3200]{1,0:T(4,128)S(1)}, f32[4,3200]{1,0:T(4,128)S(1)}, u32[]{:S(2)}, u32[]{:S(2)}) collective-permute-start(f32[4,3200]{1,0:T(4,128)S(1)} %add_add_fusion.5), channel_id=1, source_target_pairs={{0,24},{4,28},{8,16},{12,20},{16,8},{20,12},{24,0},{28,4},{1,25},{... | collective-permute-start | bytes 153608 | tf_op jit(solution)/shard_map/ppermute | solution.py:194
  41.5 4.8 %collective-permute-start.18 = (f32[4,3200]{1,0:T(4,128)S(1)}, f32[4,3200]{1,0:T(4,128)S(1)}, u32[]{:S(2)}, u32[]{:S(2)}) collective-permute-start(f32[4,3200]{1,0:T(4,128)S(1)} %add_add_fusion.5), channel_id=1, source_target_pairs={{0,28},{4,24},{8,20},{12,16},{16,12},{20,8},{24,4},{28,0},{1,29},{... | collective-permute-start | bytes 153608 | tf_op jit(solution)/shard_map/ppermute | solution.py:194
  49.1 4.8 %collective-permute-start.23 = (f32[4,1536]{1,0:T(4,128)S(1)}, f32[4,1536]{1,0:T(4,128)S(1)}, u32[]{:S(2)}, u32[]{:S(2)}) collective-permute-start(f32[4,1536]{1,0:T(4,128)S(1)} %add.115), channel_id=1, source_target_pairs={{0,80},{16,64},{32,112},{48,96},{64,16},{80,0},{96,48},{112,32},{1... | collective-permute-start | bytes 73736 | tf_op jit(solution)/shard_map/ppermute | solution.py:194
  50.4 4.5 %collective-permute-start.22 = (f32[4,1536]{1,0:T(4,128)S(1)}, f32[4,1536]{1,0:T(4,128)S(1)}, u32[]{:S(2)}, u32[]{:S(2)}) collective-permute-start(f32[4,1536]{1,0:T(4,128)S(1)} %add.115), channel_id=1, source_target_pairs={{0,112},{16,96},{32,80},{48,64},{64,48},{80,32},{96,16},{112,0},{1... | collective-permute-start | bytes 73736 | tf_op jit(solution)/shard_map/ppermute | solution.py:194
  56.2 5.2 %collective-permute-start.27 = (f32[4,3200]{1,0:T(4,128)S(1)}, f32[4,3200]{1,0:T(4,128)S(1)}, u32[]{:S(2)}, u32[]{:S(2)}) collective-permute-start(f32[4,3200]{1,0:T(4,128)S(1)} %get-tuple-element.51), channel_id=1, source_target_pairs={{0,18},{1,19},{2,16},{3,17},{16,2},{17,3},{18,0},{19,1},{4,22},{5,... | collective-permute-start | bytes 153608 | tf_op jit(solution)/shard_map/ppermute | solution.py:194
  57.6 5.0 %collective-permute-start.26 = (f32[4,3200]{1,0:T(4,128)S(1)}, f32[4,3200]{1,0:T(4,128)S(1)}, u32[]{:S(2)}, u32[]{:S(2)}) collective-permute-start(f32[4,3200]{1,0:T(4,128)S(1)} %get-tuple-element.51), channel_id=1, source_target_pairs={{0,19},{1,18},{2,17},{3,16},{16,3},{17,2},{18,1},{19,0},{4,23},{5,... | collective-permute-start | bytes 153608 | tf_op jit(solution)/shard_map/ppermute | solution.py:194
  62.7 5.3 %collective-permute-start.31 = (f32[4,3200]{1,0:T(4,128)S(1)}, f32[4,3200]{1,0:T(4,128)S(1)}, u32[]{:S(2)}, u32[]{:S(2)}) collective-permute-start(f32[4,3200]{1,0:T(4,128)S(1)} %add_add_fusion.3), channel_id=1, source_target_pairs={{0,24},{4,28},{8,16},{12,20},{16,8},{20,12},{24,0},{28,4},{1,25},{... | collective-permute-start | bytes 153608 | tf_op jit(solution)/shard_map/ppermute | solution.py:194
  64.6 4.9 %collective-permute-start.30 = (f32[4,3200]{1,0:T(4,128)S(1)}, f32[4,3200]{1,0:T(4,128)S(1)}, u32[]{:S(2)}, u32[]{:S(2)}) collective-permute-start(f32[4,3200]{1,0:T(4,128)S(1)} %add_add_fusion.3), channel_id=1, source_target_pairs={{0,28},{4,24},{8,20},{12,16},{16,12},{20,8},{24,4},{28,0},{1,29},{... | collective-permute-start | bytes 153608 | tf_op jit(solution)/shard_map/ppermute | solution.py:194
  72.2 4.8 %collective-permute-start.35 = (f32[4,1536]{1,0:T(4,128)S(1)}, f32[4,1536]{1,0:T(4,128)S(1)}, u32[]{:S(2)}, u32[]{:S(2)}) collective-permute-start(f32[4,1536]{1,0:T(4,128)S(1)} %add.125), channel_id=1, source_target_pairs={{0,80},{16,64},{32,112},{48,96},{64,16},{80,0},{96,48},{112,32},{1... | collective-permute-start | bytes 73736 | tf_op jit(solution)/shard_map/ppermute | solution.py:194
  74.2 4.5 %collective-permute-start.34 = (f32[4,1536]{1,0:T(4,128)S(1)}, f32[4,1536]{1,0:T(4,128)S(1)}, u32[]{:S(2)}, u32[]{:S(2)}) collective-permute-start(f32[4,1536]{1,0:T(4,128)S(1)} %add.125), channel_id=1, source_target_pairs={{0,112},{16,96},{32,80},{48,64},{64,48},{80,32},{96,16},{112,0},{1... | collective-permute-start | bytes 73736 | tf_op jit(solution)/shard_map/ppermute | solution.py:194
  80.1 5.3 %collective-permute-start.39 = (f32[4,3200]{1,0:T(4,128)S(1)}, f32[4,3200]{1,0:T(4,128)S(1)}, u32[]{:S(2)}, u32[]{:S(2)}) collective-permute-start(f32[4,3200]{1,0:T(4,128)S(1)} %get-tuple-element.58), channel_id=1, source_target_pairs={{0,18},{1,19},{2,16},{3,17},{16,2},{17,3},{18,0},{19,1},{4,22},{5,... | collective-permute-start | bytes 153608 | tf_op jit(solution)/shard_map/ppermute | solution.py:194
  81.9 4.9 %collective-permute-start.38 = (f32[4,3200]{1,0:T(4,128)S(1)}, f32[4,3200]{1,0:T(4,128)S(1)}, u32[]{:S(2)}, u32[]{:S(2)}) collective-permute-start(f32[4,3200]{1,0:T(4,128)S(1)} %get-tuple-element.58), channel_id=1, source_target_pairs={{0,19},{1,18},{2,17},{3,16},{16,3},{17,2},{18,1},{19,0},{4,23},{5,... | collective-permute-start | bytes 153608 | tf_op jit(solution)/shard_map/ppermute | solution.py:194
  86.9 5.4 %collective-permute-start.43 = (f32[4,3200]{1,0:T(4,128)S(1)}, f32[4,3200]{1,0:T(4,128)S(1)}, u32[]{:S(2)}, u32[]{:S(2)}) collective-permute-start(f32[4,3200]{1,0:T(4,128)S(1)} %add_add_fusion.1), channel_id=1, source_target_pairs={{0,24},{4,28},{8,16},{12,20},{16,8},{20,12},{24,0},{28,4},{1,25},{... | collective-permute-start | bytes 153608 | tf_op jit(solution)/shard_map/ppermute | solution.py:194
  88.6 4.9 %collective-permute-start.42 = (f32[4,3200]{1,0:T(4,128)S(1)}, f32[4,3200]{1,0:T(4,128)S(1)}, u32[]{:S(2)}, u32[]{:S(2)}) collective-permute-start(f32[4,3200]{1,0:T(4,128)S(1)} %add_add_fusion.1), channel_id=1, source_target_pairs={{0,28},{4,24},{8,20},{12,16},{16,12},{20,8},{24,4},{28,0},{1,29},{... | collective-permute-start | bytes 153608 | tf_op jit(solution)/shard_map/ppermute | solution.py:194
  95.0 4.5 %collective-permute-start.47 = (f32[4,128]{1,0:T(4,128)S(1)}, f32[4,128]{1,0:T(4,128)S(1)}, u32[]{:S(2)}, u32[]{:S(2)}) collective-permute-start(f32[4,128]{1,0:T(4,128)S(1)} %add.135), channel_id=1, source_target_pairs={{0,80},{16,64},{32,112},{48,96},{64,16},{80,0},{96,48},{112,32},{1... | collective-permute-start | bytes 6152 | tf_op jit(solution)/shard_map/ppermute | solution.py:194
  (27 other events, 130.4 us)
